TPU v7x, 32 devices: a whole 2x2x4 slice. The times are simulated.
32 devices in a mesh: expert: 8 (over z, x), replica: 4 (over y, core).
Axes of the slice: x: 2, y: 2, z: 4, core: 2. Of those that a mesh axis runs over, the one named last changes fastest.
Arguments:
- x_tokens: bfloat16 [4096, 2048], P(('expert', 'replica')), may hold values from -6 to 6
- d_out: bfloat16 [4096, 2048], P(('expert', 'replica')), may hold values from -3 to 3
- expert_ids: int32 [4096, 2], P(('expert', 'replica')), may hold values from 0 to 7, all different within a row; in each aligned block of 128 rows (0 to 127, 128 to 255, ...) at most 64 rows name the same one
- combine: float32 [4096, 2], P(('expert', 'replica')), may hold values from 0.1 to 1
- w_stack: bfloat16 [8, 1408, 6144], P('expert'), may hold values from -0.125 to 0.125
Outputs:
- d_tokens: bfloat16 [4096, 2048], P(('expert', 'replica'))
- g_stack: bfloat16 [8, 1408, 6144], P('expert', 'replica')
Inputs may be any that keep to these rules, and one draw needn't show every extreme that they name: `expert_ids`: in the tokens of one device (aligned blocks of 128 tokens) each expert is named by at most 64 routes, and by exactly 64 in some block; a token's 2 experts differ.
All inputs are finite; a program needn't handle non-finite values.
Results may differ from a plain program's by a relative error of at most 0.013.
Values may be sent and summed in bfloat16 or wider, within the bound.
No kernel may reach another device: no remote copies, remote signals or barrier semaphores. Data moves between devices by JAX's collectives and lax.ppermute only.
A program may use at most 128 MiB of HBM per device.

v0:
```python
import jax
import jax.numpy as jnp
from jax import lax
from jax.sharding import PartitionSpec as P


def contract_rows(factor, operand):
    return lax.dot_general(
        factor, operand, (((0,), (0,)), ((), ())), preferred_element_type=jnp.float32
    )


def body(x_tokens, d_out, expert_ids, combine, w_stack):
    tok_count, feat_width = x_tokens.shape
    top_count = expert_ids.shape[1]
    expert_count = lax.axis_size("expert")
    capacity = 2 * tok_count * top_count // expert_count
    route_count = tok_count * top_count
    slot_total = expert_count * capacity
    weights = w_stack[0]
    hidden = weights.shape[0]
    w_gate = weights[:, :feat_width]
    w_up = weights[:, feat_width : 2 * feat_width]
    w_down = weights[:, 2 * feat_width :]
    flat_ids = expert_ids.reshape(route_count)
    member = (flat_ids[:, None] == jnp.arange(expert_count, dtype=jnp.int32)[None, :]).astype(
        jnp.int32
    )
    slot_rank = jnp.sum((jnp.cumsum(member, axis=0) - 1) * member, axis=1)
    slot_index = flat_ids * capacity + slot_rank
    placing = (jnp.arange(slot_total, dtype=jnp.int32)[:, None] == slot_index[None, :]).astype(
        jnp.bfloat16
    )
    x_routes = jnp.repeat(x_tokens, top_count, axis=0)
    dy_routes = (
        combine.reshape(route_count, 1) * jnp.repeat(d_out, top_count, axis=0).astype(jnp.float32)
    ).astype(jnp.bfloat16)
    send_x = jnp.dot(placing, x_routes, preferred_element_type=jnp.float32).astype(jnp.bfloat16)
    send_x = send_x.reshape(expert_count, capacity, feat_width)
    send_dy = jnp.dot(placing, dy_routes, preferred_element_type=jnp.float32).astype(jnp.bfloat16)
    send_dy = send_dy.reshape(expert_count, capacity, feat_width)
    x_slots = lax.all_to_all(send_x, "expert", split_axis=0, concat_axis=0, tiled=True)
    dy_slots = lax.all_to_all(send_dy, "expert", split_axis=0, concat_axis=0, tiled=True)
    lead_count, item_count, _ = x_slots.shape
    row_block = x_slots.reshape(lead_count * item_count, feat_width)
    grads_in = dy_slots.reshape(lead_count * item_count, feat_width)
    last_dims = (((1,), (1,)), ((), ()))
    gate_pre = lax.dot_general(row_block, w_gate, last_dims, preferred_element_type=jnp.float32)
    up_pre = lax.dot_general(row_block, w_up, last_dims, preferred_element_type=jnp.float32)
    d_hidden = lax.dot_general(grads_in, w_down, last_dims, preferred_element_type=jnp.float32)
    gate_sigmoid = jax.nn.sigmoid(gate_pre)
    gate_act = gate_pre * gate_sigmoid
    hidden_act = (gate_act * up_pre).astype(jnp.bfloat16)
    d_up = (d_hidden * gate_act).astype(jnp.bfloat16)
    d_gate = (d_hidden * up_pre * gate_sigmoid * (1.0 + gate_pre * (1.0 - gate_sigmoid))).astype(
        jnp.bfloat16
    )
    dx_rows = jnp.dot(d_gate, w_gate, preferred_element_type=jnp.float32) + jnp.dot(
        d_up, w_up, preferred_element_type=jnp.float32
    )
    dx_slots, hidden_act, d_gate, d_up, x_slots, dy_slots = (
        dx_rows.reshape(lead_count, item_count, feat_width),
        hidden_act.reshape(lead_count, item_count, hidden),
        d_gate.reshape(lead_count, item_count, hidden),
        d_up.reshape(lead_count, item_count, hidden),
        x_slots,
        dy_slots,
    )
    returned = lax.all_to_all(
        dx_slots.astype(jnp.bfloat16), "expert", split_axis=0, concat_axis=0, tiled=True
    ).astype(dx_slots.dtype)
    dx_routes = jnp.take(returned.reshape(slot_total, feat_width), slot_index, axis=0)
    d_tokens = jnp.sum(dx_routes.reshape(tok_count, top_count, feat_width), axis=1).astype(
        jnp.bfloat16
    )
    x_rows = x_slots.reshape(slot_total, feat_width)
    dy_rows = dy_slots.reshape(slot_total, feat_width)
    gate_rows = d_gate.reshape(slot_total, hidden)
    up_rows = d_up.reshape(slot_total, hidden)
    act_rows = hidden_act.reshape(slot_total, hidden)

    def part_term(factor, operand):
        return contract_rows(factor, operand)

    grad_total = lax.psum_scatter(
        jnp.concatenate(
            [
                part_term(gate_rows, x_rows),
                part_term(up_rows, x_rows),
                part_term(act_rows, dy_rows),
            ],
            axis=1,
        ).astype(jnp.bfloat16),
        "replica",
        scatter_dimension=0,
        tiled=True,
    )
    g_stack = grad_total[None]
    return (d_tokens, g_stack)


def solution(mesh):
    return jax.shard_map(
        body,
        mesh=mesh,
        in_specs=(
            P(("expert", "replica"), None),
            P(("expert", "replica"), None),
            P(("expert", "replica"), None),
            P(("expert", "replica"), None),
            P("expert", None, None),
        ),
        out_specs=(P(("expert", "replica"), None), P("expert", "replica", None)),
        check_vma=False,
    )
```

profile of v0, /device:TPU:0, one launch (start us, length us, event | category | flops | bytes accessed | tf_op | source)
XLA Modules:
  0.0 285.6 jit_solution(13681921348993128613)
XLA Ops:
  9.2 1.7 broadcast_in_dim.24
  11.3 2.0 convolution_convert_fusion.3
  13.4 7.4 %all-to-all-start.1 = ((bf16[8,64,2048]{2,1,0:T(8,128)(2,1)}), bf16[8,64,2048]{2,1,0:T(8,128)(2,1)}, u32[]{:S(2)}, u32[]{:S(2)}) async-start(bf16[8,64,2048]{2,1,0:T(8,128)(2,1)} %bitcast.5), calls=%async_computation.1 | async-start | bytes 4194304 | tf_op jit(solution)/shard_map/all_to_all | solution.py:42
  22.1 2.5 convert_element_type.44
  24.6 3.7 %convolution_convert_fusion.4 = bf16[512,2048]{1,0:T(8,128)(2,1)} fusion(f32[256,2048]{1,0:T(8,128)} %convert_element_type.44, f32[256]{0:T(256)S(1)} %mul.66, s32[256]{0:T(256)S(1)} %multiply_add_fusion), kind=kOutput, calls=%fused_computation.17 | convolution fusion | flops 539099136 | bytes 4196352 | tf_op jit(solution)/shard_map/dot_general | solution.py:40
  28.3 40.8 %all-to-all-done.1 = bf16[8,64,2048]{2,1,0:T(8,128)(2,1)} async-done(((bf16[8,64,2048]{2,1,0:T(8,128)(2,1)}), bf16[8,64,2048]{2,1,0:T(8,128)(2,1)}, u32[]{:S(2)}, u32[]{:S(2)}) %all-to-all-start.1) | async-done | bytes 2097184 | tf_op jit(solution)/shard_map/all_to_all | solution.py:42
  69.1 3.6 %all-to-all-start = ((bf16[8,64,2048]{2,1,0:T(8,128)(2,1)}), bf16[8,64,2048]{2,1,0:T(8,128)(2,1)S(1)}, u32[]{:S(2)}, u32[]{:S(2)}) async-start(bf16[8,64,2048]{2,1,0:T(8,128)(2,1)} %bitcast.2), calls=%async_computation | async-start | bytes 4194304 | tf_op jit(solution)/shard_map/all_to_all | solution.py:43
  72.9 8.3 %fusion.4 = f32[512,1408]{1,0:T(8,128)} fusion(bf16[512,2048]{1,0:T(8,128)(2,1)} %bitcast.6, bf16[1408,6144]{1,0:T(8,128)(2,1)} %bitcast.34), kind=kOutput, calls=%fused_computation.9 | convolution fusion | flops 2952790016 | bytes 10747904 | tf_op jit(solution)/shard_map/dot_general | solution.py:48
  81.2 8.3 %fusion.8 = f32[512,1408]{1,0:T(8,128)} fusion(bf16[512,2048]{1,0:T(8,128)(2,1)} %bitcast.6, bf16[1408,6144]{1,0:T(8,128)(2,1)} %bitcast.35), kind=kOutput, calls=%fused_computation.13 | convolution fusion | flops 2952790016 | bytes 10747904 | tf_op jit(solution)/shard_map/dot_general | solution.py:49
  89.5 31.6 %all-to-all-done = bf16[8,64,2048]{2,1,0:T(8,128)(2,1)S(1)} async-done(((bf16[8,64,2048]{2,1,0:T(8,128)(2,1)}), bf16[8,64,2048]{2,1,0:T(8,128)(2,1)S(1)}, u32[]{:S(2)}, u32[]{:S(2)}) %all-to-all-start) | async-done | bytes 2097184 | tf_op jit(solution)/shard_map/all_to_all | solution.py:43
  121.1 8.6 %multiply_convert_fusion.1 = (bf16[512,1408]{1,0:T(8,128)(2,1)S(1)}, bf16[512,1408]{1,0:T(8,128)(2,1)S(1)}) fusion(f32[512,1408]{1,0:T(8,128)} %fusion.4, f32[512,1408]{1,0:T(8,128)} %fusion.8, bf16[512,2048]{1,0:T(8,128)(2,1)S(1)} %bitcast.30, bf16[1408,6144]{1,0:T(8,128)(2,1)} %bitcast.36), kind=kOutput, calls=%fused_computation.19 | convolution fusion | flops 2962161664 | bytes 16515072 | tf_op jit(solution)/shard_map/dot_general | solution.py:50
  129.8 3.8 %convolution_convert_fusion = bf16[1408,2048]{1,0:T(8,128)(2,1)S(1)} fusion(bf16[512,2048]{1,0:T(8,128)(2,1)S(1)} %bitcast.31, f32[512,1408]{1,0:T(8,128)S(1)} %copy-done.4, f32[512,1408]{1,0:T(8,128)S(1)} %copy-done.3), kind=kOutput, calls=%fused_computation.2 | convolution fusion | flops 2959998976 | bytes 13631488 | tf_op jit(solution)/shard_map/dot_general | solution.py:8
  133.6 4.8 %convolution_convert_fusion.1 = bf16[1408,2048]{1,0:T(8,128)(2,1)S(1)} fusion(bf16[512,1408]{1,0:T(8,128)(2,1)S(1)} %get-tuple-element.2, bf16[512,2048]{1,0:T(8,128)(2,1)} %bitcast.6), kind=kOutput, calls=%fused_computation.3 | convolution fusion | flops 2955673600 | bytes 9306112 | tf_op jit(solution)/shard_map/dot_general | solution.py:8
  138.5 4.8 %convolution_convert_fusion.2 = bf16[1408,2048]{1,0:T(8,128)(2,1)S(1)} fusion(bf16[512,1408]{1,0:T(8,128)(2,1)S(1)} %get-tuple-element.3, bf16[512,2048]{1,0:T(8,128)(2,1)} %bitcast.6), kind=kOutput, calls=%fused_computation.4 | convolution fusion | flops 2955673600 | bytes 9306112 | tf_op jit(solution)/shard_map/dot_general | solution.py:8
  143.3 6.8 %pad_maximum_fusion = bf16[1408,6144]{1,0:T(8,128)(2,1)} fusion(bf16[1408,2048]{1,0:T(8,128)(2,1)S(1)} %convolution_convert_fusion, bf16[1408,2048]{1,0:T(8,128)(2,1)S(1)} %convolution_convert_fusion.1, bf16[1408,2048]{1,0:T(8,128)(2,1)S(1)} %convolution_convert_fusion.2), kind=kLoop, calls=%fused_computation.1 | loop fusion | flops 51904512 | bytes 34603008 | tf_op jit(solution)/shard_map/concatenate | solution.py:86
  151.4 5.5 %fusion.2 = f32[512,2048]{1,0:T(8,128)S(1)} fusion(bf16[512,1408]{1,0:T(8,128)(2,1)S(1)} %copy-done.8, bf16[1408,6144]{1,0:T(8,128)(2,1)} %bitcast.37), kind=kOutput, calls=%fused_computation.7 | convolution fusion | flops 2952790016 | bytes 11403264 | tf_op jit(solution)/shard_map/dot_general | solution.py:58
  157.0 9.0 %add_convert_fusion = bf16[512,2048]{1,0:T(8,128)(2,1)} fusion(f32[512,2048]{1,0:T(8,128)S(1)} %fusion.2, bf16[512,1408]{1,0:T(8,128)(2,1)S(1)} %copy-done.6, bf16[1408,6144]{1,0:T(8,128)(2,1)} %bitcast.38), kind=kOutput, calls=%fused_computation.15 | convolution fusion | flops 2954887168 | bytes 13500416 | tf_op jit(solution)/shard_map/dot_general | solution.py:58
  165.9 4.1 %all-to-all-start.2 = ((bf16[8,64,2048]{2,1,0:T(8,128)(2,1)}), bf16[8,64,2048]{2,1,0:T(8,128)(2,1)S(1)}, u32[]{:S(2)}, u32[]{:S(2)}) async-start(bf16[8,64,2048]{2,1,0:T(8,128)(2,1)} %bitcast.29), calls=%async_computation.2 | async-start | bytes 4194304 | tf_op jit(solution)/shard_map/all_to_all | solution.py:69
  170.7 46.9 %all-to-all-done.2 = bf16[8,64,2048]{2,1,0:T(8,128)(2,1)S(1)} async-done(((bf16[8,64,2048]{2,1,0:T(8,128)(2,1)}), bf16[8,64,2048]{2,1,0:T(8,128)(2,1)S(1)}, u32[]{:S(2)}, u32[]{:S(2)}) %all-to-all-start.2) | async-done | bytes 2097184 | tf_op jit(solution)/shard_map/all_to_all | solution.py:69
  217.6 2.6 bitcast_convert_fusion
  220.2 4.8 %gather_fusion = f32[256,2048]{1,0:T(8,128)S(1)} fusion(f32[512,2048]{1,0:T(8,128)} %bitcast_convert_fusion, s32[1024]{0:T(1024)S(1)} %pad_clamp_fusion), kind=kCustom, calls=%fused_computation | custom fusion | bytes 4195328 | tf_op jit(solution)/shard_map/jit(_take)/gather | solution.py:72
  225.0 2.2 gather.7
  227.3 5.7 %select_reduce_fusion = bf16[128,2048]{1,0:T(8,128)(2,1)} fusion(f32[128,2,2048]{2,1,0:T(2,128)} %gather.7, pred[128,2]{1,0:T(8,128)(4,1)S(1)} %copy.15), kind=kLoop, calls=%fused_computation.24 | loop fusion | flops 786432 | bytes 2621696 | tf_op jit(solution)/shard_map/reduce_sum | solution.py:73
  233.0 45.7 %reduce-scatter.2.cloned.1.call-done = bf16[352,6144]{1,0:T(8,128)(2,1)} async-done(((bf16[1408,6144]{1,0:T(8,128)(2,1)}), bf16[352,6144]{1,0:T(8,128)(2,1)}) %reduce-scatter.2.cloned.1.call-update) | async-done | bytes 4325392 | tf_op jit(solution)/shard_map/reduce_scatter | solution.py:85
  (43 shorter events, 6.0 us)
Async XLA Ops:
  13.4 7.4 %copy-start.2 = (f32[128,2]{0,1:T(2,128)S(1)}, f32[128,2]{0,1:T(2,128)}, u32[]{:S(2)}) copy-start(f32[128,2]{0,1:T(2,128)} %param.8) | copy-start | bytes 3076
  13.4 7.6 %copy-start = (bf16[128,2048]{1,0:T(8,128)(2,1)S(1)}, bf16[128,2048]{1,0:T(8,128)(2,1)}, u32[]{:S(2)}) copy-start(bf16[128,2048]{1,0:T(8,128)(2,1)} %param.6) | copy-start | bytes 1572868
  13.4 55.7 %all-to-all-start.1 = ((bf16[8,64,2048]{2,1,0:T(8,128)(2,1)}), bf16[8,64,2048]{2,1,0:T(8,128)(2,1)}, u32[]{:S(2)}, u32[]{:S(2)}) async-start(bf16[8,64,2048]{2,1,0:T(8,128)(2,1)} %bitcast.5), calls=%async_computation.1 | async-start | bytes 4194304 | tf_op jit(solution)/shard_map/all_to_all | solution.py:42
  69.1 52.1 %all-to-all-start = ((bf16[8,64,2048]{2,1,0:T(8,128)(2,1)}), bf16[8,64,2048]{2,1,0:T(8,128)(2,1)S(1)}, u32[]{:S(2)}, u32[]{:S(2)}) async-start(bf16[8,64,2048]{2,1,0:T(8,128)(2,1)} %bitcast.2), calls=%async_computation | async-start | bytes 4194304 | tf_op jit(solution)/shard_map/all_to_all | solution.py:43
  72.7 206.0 %reduce-scatter.2.cloned.1.call-start = ((), (), s32[]{:S(2)}) async-start(), calls=%async_computation.4 | async-start | bytes 21626880 | tf_op jit(solution)/shard_map/reduce_scatter | solution.py:85
  121.1 8.6 %copy-start.3 = (f32[512,1408]{1,0:T(8,128)S(1)}, f32[512,1408]{1,0:T(8,128)}, u32[]{:S(2)}) copy-start(f32[512,1408]{1,0:T(8,128)} %fusion.4) | copy-start | bytes 8650756
  121.1 8.6 %copy-start.4 = (f32[512,1408]{1,0:T(8,128)S(1)}, f32[512,1408]{1,0:T(8,128)}, u32[]{:S(2)}) copy-start(f32[512,1408]{1,0:T(8,128)} %fusion.8) | copy-start | bytes 8650756
  129.8 3.8 %copy-start.5 = (bf16[512,1408]{1,0:T(8,128)(2,1)}, bf16[512,1408]{1,0:T(8,128)(2,1)S(1)}, u32[]{:S(2)}) copy-start(bf16[512,1408]{1,0:T(8,128)(2,1)S(1)} %get-tuple-element.2) | copy-start | bytes 4325380
  129.8 8.6 %copy-start.7 = (bf16[512,1408]{1,0:T(8,128)(2,1)}, bf16[512,1408]{1,0:T(8,128)(2,1)S(1)}, u32[]{:S(2)}) copy-start(bf16[512,1408]{1,0:T(8,128)(2,1)S(1)} %get-tuple-element.3) | copy-start | bytes 4325380
  150.1 1.4 copy-start.8
  151.4 5.5 %copy-start.6 = (bf16[512,1408]{1,0:T(8,128)(2,1)S(1)}, bf16[512,1408]{1,0:T(8,128)(2,1)}, u32[]{:S(2)}) copy-start(bf16[512,1408]{1,0:T(8,128)(2,1)} %copy-done.5) | copy-start | bytes 4325380
  165.9 4.3 %copy-start.1 = (s32[128,2]{0,1:T(2,128)S(1)}, s32[128,2]{0,1:T(2,128)}, u32[]{:S(2)}) copy-start(s32[128,2]{0,1:T(2,128)} %param.7) | copy-start | bytes 3076
  165.9 51.6 %all-to-all-start.2 = ((bf16[8,64,2048]{2,1,0:T(8,128)(2,1)}), bf16[8,64,2048]{2,1,0:T(8,128)(2,1)S(1)}, u32[]{:S(2)}, u32[]{:S(2)}) async-start(bf16[8,64,2048]{2,1,0:T(8,128)(2,1)} %bitcast.29), calls=%async_computation.2 | async-start | bytes 4194304 | tf_op jit(solution)/shard_map/all_to_all | solution.py:69
Sparse Core Ops, SparseCore 0:
  150.2 128.4 reduce-scatter.1
where the time goes:
time: 286 us
  waiting for transfers between devices  165 us (58%)
  matrix products  58.9 us (21%)
  local copies, waits for them, and re-layouts  16.2 us (6%)
  other arithmetic  15.9 us (6%)
  starting transfers between devices  15.3 us (5%)
  between operations  14.3 us (5%)
    all_to_all x1, waiting for transfers between devices, body(): lax.all_to_all(dx_slots.astype(jnp.bfloat16), 'expert', split_axis=0, con...  46.9 us
    reduce_scatter x1, waiting for transfers between devices, body(): lax.psum_scatter(jnp.concatenate([part_term(gate_rows, x_rows), part_term...  45.7 us
    all_to_all x1, waiting for transfers between devices, body(): lax.all_to_all(send_x, 'expert', split_axis=0, concat_axis=0, tiled=True)  40.8 us
    all_to_all x1, waiting for transfers between devices, body(): lax.all_to_all(send_dy, 'expert', split_axis=0, concat_axis=0, tiled=True)  31.6 us
    dot_general x3, matrix products, contract_rows(): lax.dot_general(factor, operand, (((0,), (0,)), ((), ())), preferred_elem...  13.4 us
    dot_general x1, matrix products, body(): jnp.dot(d_up, w_up, preferred_element_type=jnp.float32)  8.96 us
    dot_general x1, matrix products, body(): lax.dot_general(grads_in, w_down, last_dims, preferred_element_type=jnp.f...  8.63 us
    dot_general x1, matrix products, body(): lax.dot_general(row_block, w_gate, last_dims, preferred_element_type=jnp....  8.3 us
  transfers between devices with their start and end apart: 4, of which 4 were waited for; matrix products, arithmetic and copies ran while one was open for 19% of the time, Pallas kernels for 0%

commit v1 on v0

v1 whole, which is shorter than its diff:
```python
import functools

import jax
import jax.numpy as jnp
from jax import lax
from jax.experimental import pallas as pl
from jax.experimental.pallas import tpu as pltpu
from jax.sharding import PartitionSpec as P

BF16 = jnp.bfloat16
F32 = jnp.float32
RING = (0, 1, 3, 2)
VMEM_LIMIT = 56 * 1024 * 1024


def params():
    return pltpu.CompilerParams(vmem_limit_bytes=VMEM_LIMIT)


def whole_vmem():
    return pl.BlockSpec(memory_space=pltpu.VMEM)


def smem():
    return pl.BlockSpec(memory_space=pltpu.SMEM)


def placing_of(place_ref, meta_ref, column_count, capacity):
    tokens = meta_ref.shape[1]
    base, own = place_ref[0], place_ref[1]
    id_first, id_second = meta_ref[0:1, :], meta_ref[1:2, :]
    scale_first, scale_second = meta_ref[2:3, :], meta_ref[3:4, :]
    row = lax.broadcasted_iota(jnp.int32, (16, tokens), 0)
    expert = (base + jnp.bitwise_xor(row, own)).astype(F32)
    first = id_first == expert
    member = jnp.where(first | (id_second == expert), 1.0, 0.0)
    scale = jnp.where(first, scale_first, scale_second)
    earlier = lax.broadcasted_iota(jnp.int32, (tokens, tokens), 0)
    later = lax.broadcasted_iota(jnp.int32, (tokens, tokens), 1)
    before = jnp.where(earlier < later, 1.0, 0.0).astype(BF16)
    rank = jnp.dot(member.astype(BF16), before, preferred_element_type=F32)
    rank = jnp.where(member > 0.0, rank, -1.0)
    slot = lax.broadcasted_iota(jnp.int32, (capacity, tokens), 0).astype(F32)
    hits, scales = [], []
    for d in range(column_count):
        hit = jnp.where(rank[d : d + 1, :] == slot, 1.0, 0.0)
        hits.append(hit)
        scales.append(jnp.sum(hit * scale[d : d + 1, :], axis=1, keepdims=True))
    return jnp.concatenate(hits, axis=0), jnp.concatenate(scales, axis=0)


def select_kernel(column_count, capacity, scaled, place_ref, meta_ref, rows_ref, *out_refs):
    hits, scales = placing_of(place_ref, meta_ref, column_count, capacity)
    picked = jnp.dot(hits.astype(BF16), rows_ref[...], preferred_element_type=F32)
    if scaled:
        picked = picked * scales
    picked = picked.astype(BF16)
    for d in range(column_count):
        out_refs[d][...] = picked[d * capacity : (d + 1) * capacity, :]


def select(place, meta, rows, column_count, capacity, scaled):
    tokens, width = rows.shape
    return pl.pallas_call(
        functools.partial(select_kernel, column_count, capacity, scaled),
        out_shape=[jax.ShapeDtypeStruct((capacity, width), BF16)] * column_count,
        in_specs=[smem(), whole_vmem(), whole_vmem()],
        out_specs=[whole_vmem()] * column_count,
        compiler_params=params(),
        cost_estimate=pl.CostEstimate(
            flops=2 * column_count * capacity * tokens * width,
            bytes_accessed=4 * tokens * width,
            transcendentals=0,
        ),
        name="select_scaled" if scaled else "select",
    )(place, meta, rows)


def merge_kernel(column_count, capacity, has_carry, place_ref, meta_ref, *refs):
    parts = refs[:column_count]
    out_ref = refs[-1]
    hits, _ = placing_of(place_ref, meta_ref, column_count, capacity)
    slots = jnp.concatenate([part[...] for part in parts], axis=0)
    total = lax.dot_general(
        hits.astype(BF16), slots, (((0,), (0,)), ((), ())), preferred_element_type=F32
    )
    if has_carry:
        total = total + refs[column_count][...].astype(F32)
    out_ref[...] = total.astype(BF16)


def merge(place, meta, parts, carry):
    column_count, (capacity, width) = len(parts), parts[0].shape
    tokens = meta.shape[1]
    operands = [place, meta, *parts] + ([] if carry is None else [carry])
    return pl.pallas_call(
        functools.partial(merge_kernel, column_count, capacity, carry is not None),
        out_shape=jax.ShapeDtypeStruct((tokens, width), BF16),
        in_specs=[smem()] + [whole_vmem()] * (len(operands) - 1),
        out_specs=whole_vmem(),
        compiler_params=params(),
        cost_estimate=pl.CostEstimate(
            flops=2 * column_count * capacity * tokens * width,
            bytes_accessed=6 * tokens * width,
            transcendentals=0,
        ),
        name="merge",
    )(*operands)


def expert_kernel(chunk_count, capacity, half_ref, *refs):
    x_refs, refs = refs[:chunk_count], refs[chunk_count:]
    dy_refs, refs = refs[:chunk_count], refs[chunk_count:]
    w_ref, send_ref, keep_ref, hid_ref = refs[:4]
    dx_refs, (x_all, dy_all, acc) = refs[4:-3], refs[-3:]
    step = pl.program_id(0)
    width = x_all.shape[1]
    chunk_rows = x_refs[0].shape[0]

    @pl.when(step == 0)
    def _():
        for i in range(chunk_count):
            x_all[i * chunk_rows : (i + 1) * chunk_rows, :] = x_refs[i][...]
            dy_all[i * chunk_rows : (i + 1) * chunk_rows, :] = dy_refs[i][...]

    last = (((1,), (1,)), ((), ()))
    first = (((0,), (0,)), ((), ()))
    x, dy = x_all[...], dy_all[...]
    gate = lax.dot_general(w_ref[0, :, :width], x, last, preferred_element_type=F32)
    up = lax.dot_general(w_ref[0, :, width : 2 * width], x, last, preferred_element_type=F32)
    d_hidden = lax.dot_general(w_ref[0, :, 2 * width :], dy, last, preferred_element_type=F32)
    sig = jax.nn.sigmoid(gate)
    act = gate * sig
    hid_ref[0] = (act * up).astype(BF16)
    d_up = (d_hidden * act).astype(BF16)
    d_gate = (d_hidden * up * sig * (1.0 + gate * (1.0 - sig))).astype(BF16)

    @pl.when(step == 0)
    def _():
        send_ref[0] = d_gate
        send_ref[1] = d_up

    @pl.when(step == 1)
    def _():
        keep_ref[0] = d_gate
        keep_ref[1] = d_up

    part = lax.dot_general(
        d_gate, w_ref[0, :, :width], first, preferred_element_type=F32
    ) + lax.dot_general(
        d_up, w_ref[0, :, width : 2 * width], first, preferred_element_type=F32
    )

    @pl.when(step == 0)
    def _():
        acc[...] = part

    @pl.when(step == 1)
    def _():
        total = (acc[...] + part).astype(BF16)
        for i in range(len(dx_refs)):
            dx_refs[i][...] = total[i * capacity : (i + 1) * capacity, :]


def expert(half, x_chunks, dy_chunks, w_stack, capacity):
    chunk_count = len(x_chunks)
    chunk_rows, width = x_chunks[0].shape
    rows = chunk_count * chunk_rows
    hidden = w_stack.shape[1]
    part = hidden // 2
    chunk_spec = pl.BlockSpec((chunk_rows, width), lambda j, h: (0, 0))
    pair_spec = pl.BlockSpec((2, part, rows), lambda j, h: (0, 0, 0))

    def half_of(j, h):
        return jnp.bitwise_xor(h[0], 1 - j)

    piece_count = rows // capacity
    outs = pl.pallas_call(
        functools.partial(expert_kernel, chunk_count, capacity),
        grid_spec=pltpu.PrefetchScalarGridSpec(
            num_scalar_prefetch=1,
            grid=(2,),
            in_specs=[chunk_spec] * (2 * chunk_count)
            + [pl.BlockSpec((1, part, 3 * width), lambda j, h: (0, half_of(j, h), 0))],
            out_specs=[
                pair_spec,
                pair_spec,
                pl.BlockSpec((1, part, rows), lambda j, h: (half_of(j, h), 0, 0)),
            ]
            + [pl.BlockSpec((capacity, width), lambda j, h: (0, 0))] * piece_count,
            scratch_shapes=[
                pltpu.VMEM((rows, width), BF16),
                pltpu.VMEM((rows, width), BF16),
                pltpu.VMEM((rows, width), F32),
            ],
        ),
        out_shape=[
            jax.ShapeDtypeStruct((2, part, rows), BF16),
            jax.ShapeDtypeStruct((2, part, rows), BF16),
            jax.ShapeDtypeStruct((2, part, rows), BF16),
        ]
        + [jax.ShapeDtypeStruct((capacity, width), BF16)] * piece_count,
        compiler_params=params(),
        cost_estimate=pl.CostEstimate(
            flops=10 * rows * width * hidden,
            bytes_accessed=6 * width * hidden + 6 * rows * width + 6 * rows * hidden,
            transcendentals=rows * hidden,
        ),
        name="expert",
    )(half, *x_chunks, *dy_chunks, w_stack)
    return outs[0], outs[1], outs[2], outs[3:]


def grad_kernel(act_count, row_count, add_axes, pick_ref, *refs):
    acts, refs = refs[:act_count], refs[act_count:]
    rows, refs = refs[:row_count], refs[row_count:]
    adds, out_ref = refs[: len(add_axes)], refs[-1]
    left = jnp.concatenate([ref[0] for ref in acts], axis=1)
    right = jnp.concatenate([ref[...] for ref in rows], axis=0)
    total = jnp.dot(left, right, preferred_element_type=F32)
    for ref, axes in zip(adds, add_axes):
        total = total + (ref[...] if axes == 2 else ref[0]).astype(F32)
    out_ref[...] = total.astype(BF16).reshape(out_ref.shape)


def grad(pick, leads, acts, rows, adds, out_shape, first_column, into=None, name="grad"):
    own = acts[0].shape[1] // 2
    width = rows[0].shape[1]
    tile = min(1024, width)
    tiles = width // tile
    lead_count = 1 if leads is None else leads
    stacked = len(out_shape) == 3

    def lead_of(i, pick_ref):
        return pick_ref[0] if leads is None else i

    in_specs = [
        pl.BlockSpec((1, own, act.shape[2]), lambda i, n, s: (lead_of(i, s), s[1], 0))
        for act in acts
    ] + [pl.BlockSpec((row.shape[0], tile), lambda i, n, s: (0, n)) for row in rows]
    operands = list(acts) + list(rows)
    add_axes = []
    for add in adds:
        operands.append(add)
        add_axes.append(add.ndim)
        if add.ndim == 3:
            in_specs.append(
                pl.BlockSpec((1, own, tile), lambda i, n, s: (lead_of(i, s), 0, n))
            )
        else:
            in_specs.append(pl.BlockSpec((own, tile), lambda i, n, s: (0, i * tiles + n)))
    aliases = {}
    kernel = functools.partial(grad_kernel, len(acts), len(rows), tuple(add_axes))
    if into is not None:
        operands.append(into)
        in_specs.append(pl.BlockSpec(memory_space=pl.ANY))
        aliases = {len(operands): 0}
        inner = kernel

        def kernel(pick_ref, *refs):
            inner(pick_ref, *refs[:-2], refs[-1])

    if stacked:
        out_spec = pl.BlockSpec((1, own, tile), lambda i, n, s: (i, 0, n))
    else:
        out_spec = pl.BlockSpec(
            (own, tile), lambda i, n, s: (0, first_column // tile + i * tiles + n)
        )
    depth = sum(act.shape[2] for act in acts)
    return pl.pallas_call(
        kernel,
        grid_spec=pltpu.PrefetchScalarGridSpec(
            num_scalar_prefetch=1,
            grid=(lead_count, tiles),
            in_specs=in_specs,
            out_specs=out_spec,
        ),
        out_shape=jax.ShapeDtypeStruct(out_shape, BF16),
        input_output_aliases=aliases,
        compiler_params=params(),
        cost_estimate=pl.CostEstimate(
            flops=2 * lead_count * own * depth * width,
            bytes_accessed=2 * depth * width + 2 * lead_count * own * (depth + 2 * width),
            transcendentals=0,
        ),
        name=name,
    )(pick, *operands)


def body(x_tokens, d_out, expert_ids, combine, w_stack):
    tokens, width = x_tokens.shape
    experts = lax.axis_size("expert")
    replicas = lax.axis_size("replica")
    plane_count = len(RING)
    columns = experts // plane_count
    capacity = 2 * tokens * expert_ids.shape[1] // experts
    hidden = w_stack.shape[1]
    own_rows = hidden // replicas

    position = lax.axis_index("expert")
    replica = lax.axis_index("replica")
    plane, column = position // columns, position % columns
    high, low = replica // 2, replica % 2
    place = jnp.stack([plane * columns, column]).astype(jnp.int32)
    half = high.reshape(1).astype(jnp.int32)

    follower = {RING[i]: RING[(i + 1) % plane_count] for i in range(plane_count)}
    ring_pairs = [
        (p * columns + c, follower[p] * columns + c)
        for p in range(plane_count)
        for c in range(columns)
    ]

    def along_ring(value):
        return lax.ppermute(value, "expert", ring_pairs)

    def across_columns(value, d):
        pairs = [
            (p * columns + c, p * columns + (c ^ d))
            for p in range(plane_count)
            for c in range(columns)
        ]
        return lax.ppermute(value, "expert", pairs)

    def across_replicas(value, d):
        return lax.ppermute(value, "replica", [(r, r ^ d) for r in range(replicas)])

    meta = jnp.concatenate([expert_ids.T.astype(F32), combine.T], axis=0)
    metas, x_blocks, d_blocks = [meta], [x_tokens], [d_out]
    for _ in range(plane_count - 1):
        metas.append(along_ring(metas[-1]))
        x_blocks.append(along_ring(x_blocks[-1]))
        d_blocks.append(along_ring(d_blocks[-1]))

    def chunk_of(block, meta_rows, scaled):
        picked = select(place, meta_rows, block, columns, capacity, scaled)
        arrived = [picked[0]] + [across_columns(picked[d], d) for d in range(1, columns)]
        return jnp.concatenate(arrived, axis=0)

    x_chunks, dy_chunks, x_other = [], [], []
    for s in range(plane_count):
        x_chunks.append(chunk_of(x_blocks[s], metas[s], False))
        x_other.append(across_replicas(x_chunks[s], 2))
        dy_chunks.append(chunk_of(d_blocks[s], metas[s], True))

    keeps, sends, hids, pieces = [], [], [], []
    group = 2
    for g in range(0, plane_count, group):
        send, keep, hid, dx = expert(
            half, x_chunks[g : g + group], dy_chunks[g : g + group], w_stack, capacity
        )
        keeps.append(keep)
        sends.append(across_replicas(send, 2))
        hids.append(hid)
        pieces.extend(dx)

    def dx_parts(s):
        mine = pieces[s * columns : (s + 1) * columns]
        return [mine[0]] + [across_columns(mine[d], d) for d in range(1, columns)]

    carry = None
    for s in range(1, plane_count):
        carry = along_ring(merge(place, metas[s], dx_parts(s), carry))
    d_tokens = merge(place, metas[0], dx_parts(0), carry)

    def pick(lead, rows):
        return jnp.stack([lead, rows]).astype(jnp.int32)

    down_shape = (2, own_rows, width)
    down_cores = across_replicas(
        grad(pick(high, 1 - low), 2, hids, dy_chunks, [], down_shape, 0, name="grad_down_core"), 1
    )
    down_y = across_replicas(
        grad(
            pick(1 - high, low), None, hids, dy_chunks, [down_cores], (own_rows, width), 0,
            name="grad_down_y",
        ),
        2,
    )
    acts, rows = keeps + sends, x_chunks + x_other
    x_cores = across_replicas(
        grad(pick(high, 1 - low), 2, acts, rows, [], (own_rows, 2 * width), 0, name="grad_x_core"),
        1,
    )
    g_rows = grad(
        pick(high, low), 2, acts, rows, [x_cores], (own_rows, 3 * width), 0, name="grad_x_own"
    )
    g_rows = grad(
        pick(high, low), None, hids, dy_chunks, [down_cores, down_y], (own_rows, 3 * width),
        2 * width, into=g_rows, name="grad_down_own",
    )
    return d_tokens, g_rows[None]


def solution(mesh):
    return jax.shard_map(
        body,
        mesh=mesh,
        in_specs=(
            P(("expert", "replica"), None),
            P(("expert", "replica"), None),
            P(("expert", "replica"), None),
            P(("expert", "replica"), None),
            P("expert", None, None),
        ),
        out_specs=(P(("expert", "replica"), None), P("expert", "replica", None)),
        check_vma=False,
    )
```

time: 286 us -> 287 us (level)
  Pallas kernels: 0 us -> 104 us
  matrix products: 58.9 us -> 0 us
  waiting for transfers between devices: 165 us -> 122 us
  starting transfers between devices: 15.3 us -> 35 us
  between operations: 14.3 us -> 1.07 us
  other arithmetic: 15.9 us -> 3.8 us
  local copies, waits for them, and re-layouts: 16.2 us -> 21.2 us
    ppermute x0 -> x33, waiting for transfers between devices: none -> 122 us  [the longest x9 52.4 us: across_replicas(): return lax.ppermute(value, 'replica', [(r, r ^ d) for r in range(replicas)])]
    all_to_all x3 -> x0, waiting for transfers between devices: 119 us -> none  [the longest x1 46.9 us: body(): lax.all_to_all(dx_slots.astype(jnp.bfloat16), 'expert', split_axis=0, con...]
    pallas_call x0 -> x19, Pallas kernels: none -> 104 us  [the longest x2 42.4 us: expert(): pl.pallas_call(functools.partial(expert_kernel, chunk_count, capacity), g...]
    dot_general x10 -> x0, matrix products: 58.9 us -> none  [the longest x3 13.4 us: contract_rows(): lax.dot_general(factor, operand, (((0,), (0,)), ((), ())), preferred_elem...]
    reduce_scatter x1 -> x0, waiting for transfers between devices: 45.7 us -> none  [body(): lax.psum_scatter(jnp.concatenate([part_term(gate_rows, x_rows), part_term...]
    ppermute x0 -> x33, starting transfers between devices: none -> 35 us  [the longest x12 16.4 us: across_columns(): return lax.ppermute(value, 'expert', pairs)]
    unnamed x20 -> x84, local copies, waits for them, and re-layouts: 2.27 us -> 21.1 us
    all_to_all x3 -> x0, starting transfers between devices: 15.1 us -> none  [the longest x1 7.38 us: body(): lax.all_to_all(send_x, 'expert', split_axis=0, concat_axis=0, tiled=True)]
  transfers between devices with their start and end apart: 4 -> 33, of which waited for: 4 -> 15; matrix products, arithmetic and copies ran while one was open for 19% -> 4% of each run, Pallas kernels for 0% -> 35%
where the time goes in v1:
time: 287 us
  waiting for transfers between devices  122 us (43%)
  Pallas kernels  104 us (36%)
  starting transfers between devices  35 us (12%)
  local copies, waits for them, and re-layouts  21.2 us (7%)
  other arithmetic  3.8 us (1%)
    ppermute x9, waiting for transfers between devices, across_replicas(): return lax.ppermute(value, 'replica', [(r, r ^ d) for r in range(replicas)])  52.4 us
    ppermute x12, waiting for transfers between devices, along_ring(): return lax.ppermute(value, 'expert', ring_pairs)  42.6 us
    pallas_call x2, Pallas kernels, expert(): pl.pallas_call(functools.partial(expert_kernel, chunk_count, capacity), g...  42.4 us
    pallas_call x5, Pallas kernels, grad(): pl.pallas_call(kernel, grid_spec=pltpu.PrefetchScalarGridSpec(num_scalar_...  33.4 us
    ppermute x12, waiting for transfers between devices, across_columns(): return lax.ppermute(value, 'expert', pairs)  26.9 us
    unnamed x84, local copies, waits for them, and re-layouts  21.1 us
    pallas_call x8, Pallas kernels, select(): pl.pallas_call(functools.partial(select_kernel, column_count, capacity, s...  18 us
    ppermute x12, starting transfers between devices, across_columns(): return lax.ppermute(value, 'expert', pairs)  16.4 us
  transfers between devices with their start and end apart: 33, of which 15 were waited for; matrix products, arithmetic and copies ran while one was open for 4% of the time, Pallas kernels for 35%

profile of v1, /device:TPU:0, one launch (start us, length us, event | category | flops | bytes accessed | tf_op | source)
XLA Modules:
  0.0 286.6 jit_solution(17033312790511698245)
XLA Ops:
  2.0 3.0 %collective-permute-start.1 = (f32[4,128]{1,0:T(4,128)S(1)}, f32[4,128]{1,0:T(4,128)S(1)}, u32[]{:S(2)}, u32[]{:S(2)}) collective-permute-start(f32[4,128]{1,0:T(4,128)S(1)} %pad_maximum_fusion.meta_ref), channel_id=1, source_target_pairs={{0,8},{4,12},{8,24},{12,28},{16,0},{20,4},{24,16},{28,20},{1,9},{5... | collective-permute-start | bytes 6152 | tf_op jit(solution)/shard_map/ppermute | solution.py:315
  5.0 2.6 collective-permute-start.2
  17.9 12.9 %collective-permute-done.8.meta_ref = f32[4,128]{1,0:T(4,128)S(1)} collective-permute-done((f32[4,128]{1,0:T(4,128)S(1)}, f32[4,128]{1,0:T(4,128)S(1)}, u32[]{:S(2)}, u32[]{:S(2)}) %collective-permute-start.8) | collective-permute-done | bytes 2080 | tf_op jit(solution)/shard_map/ppermute | solution.py:315
  45.9 3.6 %collective-permute-done.6 = bf16[64,2048]{1,0:T(8,128)(2,1)S(1)} collective-permute-done((bf16[64,2048]{1,0:T(8,128)(2,1)}, bf16[64,2048]{1,0:T(8,128)(2,1)S(1)}, u32[]{:S(2)}, u32[]{:S(2)}) %collective-permute-start.6) | collective-permute-done | bytes 262176 | tf_op jit(solution)/shard_map/ppermute | solution.py:323
  50.3 21.2 %expert.2 = (bf16[2,704,256]{2,1,0:T(8,128)(2,1)}, bf16[2,704,256]{2,1,0:T(8,128)(2,1)}, bf16[2,704,256]{2,1,0:T(8,128)(2,1)}, bf16[64,2048]{1,0:T(8,128)(2,1)},...) custom-call(s32[1]{0:T(128)} %bitcast.4.half_ref, bf16[128,2048]{1,0:T(8,128)(2,1)} %copy-done.6, ...), custom_call_target="tpu_custom_call" | custom-call | flops 7381975040 | bytes 22609920 | tf_op jit(solution)/shard_map/expert/pallas_call | solution.py:178
  83.5 3.3 %collective-permute-done.11 = bf16[64,2048]{1,0:T(8,128)(2,1)S(1)} collective-permute-done((bf16[64,2048]{1,0:T(8,128)(2,1)}, bf16[64,2048]{1,0:T(8,128)(2,1)S(1)}, u32[]{:S(2)}, u32[]{:S(2)}) %collective-permute-start.11) | collective-permute-done | bytes 262176 | tf_op jit(solution)/shard_map/ppermute | solution.py:323
  87.3 9.3 %collective-permute-done.12.rows_ref = bf16[128,2048]{1,0:T(8,128)(2,1)S(1)} collective-permute-done((bf16[128,2048]{1,0:T(8,128)(2,1)}, bf16[128,2048]{1,0:T(8,128)(2,1)S(1)}, u32[]{:S(2)}, u32[]{:S(2)}) %collective-permute-start.12) | collective-permute-done | bytes 524320 | tf_op jit(solution)/shard_map/ppermute | solution.py:315
  110.0 3.8 %collective-permute-done.17 = bf16[64,2048]{1,0:T(8,128)(2,1)S(1)} collective-permute-done((bf16[64,2048]{1,0:T(8,128)(2,1)}, bf16[64,2048]{1,0:T(8,128)(2,1)S(1)}, u32[]{:S(2)}, u32[]{:S(2)}) %collective-permute-start.17) | collective-permute-done | bytes 262176 | tf_op jit(solution)/shard_map/ppermute | solution.py:323
  114.7 21.2 %expert.3 = (bf16[2,704,256]{2,1,0:T(8,128)(2,1)}, bf16[2,704,256]{2,1,0:T(8,128)(2,1)}, bf16[2,704,256]{2,1,0:T(8,128)(2,1)}, bf16[64,2048]{1,0:T(8,128)(2,1)},...) custom-call(s32[1]{0:T(128)} %bitcast.4.half_ref, bf16[128,2048]{1,0:T(8,128)(2,1)} %copy-done.8, ...), custom_call_target="tpu_custom_call" | custom-call | flops 7381975040 | bytes 22609920 | tf_op jit(solution)/shard_map/expert/pallas_call | solution.py:178
  135.9 6.6 %grad_down_core.1 = bf16[2,352,2048]{2,1,0:T(8,128)(2,1)} custom-call(s32[2]{0:T(128)} %pad_add_fusion.1.pick_ref, bf16[2,704,256]{2,1,0:T(8,128)(2,1)} %get-tuple-element.56.refs_0_, bf16[2,704,256]{2,1,0:T(8,128)(2,1)} %get-tuple-element.57.refs_1_, bf16[128,2048]{1,0:T(8,128)(2,1)} %copy-done.1, bf16[128,2048]{1,0:T(8,128)(2,1)} %copy-done.3, ...), custom_call_target="tpu_custom_call" | custom-call | flops 1476395008 | bytes 8585216 | tf_op jit(solution)/shard_map/grad_down_core/pallas_call | solution.py:270
  146.8 15.0 %collective-permute-done.26.refs_2_ = bf16[2,704,256]{2,1,0:T(8,128)(2,1)S(1)} collective-permute-done((bf16[2,704,256]{2,1,0:T(8,128)(2,1)}, bf16[2,704,256]{2,1,0:T(8,128)(2,1)S(1)}, u32[]{:S(2)}, u32[]{:S(2)}) %collective-permute-start.26) | collective-permute-done | bytes 720928 | tf_op jit(solution)/shard_map/ppermute | solution.py:326
  161.7 26.7 %collective-permute-done.30.refs_10_ = bf16[128,2048]{1,0:T(8,128)(2,1)S(1)} collective-permute-done((bf16[128,2048]{1,0:T(8,128)(2,1)S(1)}, bf16[128,2048]{1,0:T(8,128)(2,1)S(1)}, u32[]{:S(2)}, u32[]{:S(2)}) %collective-permute-start.30) | collective-permute-done | bytes 524320 | tf_op jit(solution)/shard_map/ppermute | solution.py:326
  188.4 10.8 %collective-permute-done.31.refs_11_ = bf16[128,2048]{1,0:T(8,128)(2,1)S(1)} collective-permute-done((bf16[128,2048]{1,0:T(8,128)(2,1)S(1)}, bf16[128,2048]{1,0:T(8,128)(2,1)S(1)}, u32[]{:S(2)}, u32[]{:S(2)}) %collective-permute-start.31) | collective-permute-done | bytes 524320 | tf_op jit(solution)/shard_map/ppermute | solution.py:326
  200.3 8.7 %grad_x_core.1 = bf16[352,4096]{1,0:T(8,128)(2,1)} custom-call(s32[2]{0:T(128)} %pad_add_fusion.1.pick_ref, bf16[2,704,256]{2,1,0:T(8,128)(2,1)} %get-tuple-element.58.refs_0_, bf16[2,704,256]{2,1,0:T(8,128)(2,1)} %get-tuple-element.59.refs_1_, bf16[2,704,256]{2,1,0:T(8,128)(2,1)} %copy-done.12, bf16[2,704,256]{2,1,0:T(8,128)(2,1)} %copy-done.13, ...), custom_call_target="tpu_custom_call" | custom-call | flops 2952790016 | bytes 11403264 | tf_op jit(solution)/shard_map/grad_x_core/pallas_call | solution.py:270
  210.9 6.9 %collective-permute-done.20.refs_1_ = bf16[64,2048]{1,0:T(8,128)(2,1)S(1)} collective-permute-done((bf16[64,2048]{1,0:T(8,128)(2,1)S(1)}, bf16[64,2048]{1,0:T(8,128)(2,1)S(1)}, u32[]{:S(2)}, u32[]{:S(2)}) %collective-permute-start.20) | collective-permute-done | bytes 262176 | tf_op jit(solution)/shard_map/ppermute | solution.py:323
  225.2 4.4 %grad_down_y.1 = bf16[352,2048]{1,0:T(8,128)(2,1)} custom-call(s32[2]{0:T(128)} %pad_add_fusion.2.pick_ref, bf16[2,704,256]{2,1,0:T(8,128)(2,1)} %get-tuple-element.56.refs_0_, bf16[2,704,256]{2,1,0:T(8,128)(2,1)} %get-tuple-element.57.refs_1_, bf16[128,2048]{1,0:T(8,128)(2,1)} %copy-done.1, bf16[128,2048]{1,0:T(8,128)(2,1)} %copy-done.3, ...), custom_call_target="tpu_custom_call" | custom-call | flops 738197504 | bytes 5341184 | tf_op jit(solution)/shard_map/grad_down_y/pallas_call | solution.py:270
  230.1 5.3 %collective-permute-done.21.refs_2_ = bf16[128,2048]{1,0:T(8,128)(2,1)S(1)} collective-permute-done((bf16[128,2048]{1,0:T(8,128)(2,1)}, bf16[128,2048]{1,0:T(8,128)(2,1)S(1)}, u32[]{:S(2)}, u32[]{:S(2)}) %collective-permute-start.21) | collective-permute-done | bytes 524320 | tf_op jit(solution)/shard_map/ppermute | solution.py:315
  240.5 5.2 %collective-permute-done.18.refs_1_ = bf16[64,2048]{1,0:T(8,128)(2,1)S(1)} collective-permute-done((bf16[64,2048]{1,0:T(8,128)(2,1)S(1)}, bf16[64,2048]{1,0:T(8,128)(2,1)S(1)}, u32[]{:S(2)}, u32[]{:S(2)}) %collective-permute-start.18) | collective-permute-done | bytes 262176 | tf_op jit(solution)/shard_map/ppermute | solution.py:323
  245.8 6.7 %collective-permute-done.22.refs_2_ = bf16[128,2048]{1,0:T(8,128)(2,1)S(1)} collective-permute-done((bf16[128,2048]{1,0:T(8,128)(2,1)}, bf16[128,2048]{1,0:T(8,128)(2,1)S(1)}, u32[]{:S(2)}, u32[]{:S(2)}) %collective-permute-start.22) | collective-permute-done | bytes 524320 | tf_op jit(solution)/shard_map/ppermute | solution.py:315
  258.1 4.0 %collective-permute-done.7.refs_1_ = bf16[64,2048]{1,0:T(8,128)(2,1)S(1)} collective-permute-done((bf16[64,2048]{1,0:T(8,128)(2,1)S(1)}, bf16[64,2048]{1,0:T(8,128)(2,1)S(1)}, u32[]{:S(2)}, u32[]{:S(2)}) %collective-permute-start.7) | collective-permute-done | bytes 262176 | tf_op jit(solution)/shard_map/ppermute | solution.py:323
  262.1 6.3 %collective-permute-done.23.refs_2_ = bf16[128,2048]{1,0:T(8,128)(2,1)S(1)} collective-permute-done((bf16[128,2048]{1,0:T(8,128)(2,1)}, bf16[128,2048]{1,0:T(8,128)(2,1)S(1)}, u32[]{:S(2)}, u32[]{:S(2)}) %collective-permute-start.23) | collective-permute-done | bytes 524320 | tf_op jit(solution)/shard_map/ppermute | solution.py:315
  269.3 2.5 merge.7
  271.8 9.0 %grad_x_own.1.refs_8_ = bf16[352,6144]{1,0:T(8,128)(2,1)} custom-call(s32[2]{0:T(128)} %pad_add_fusion.3.pick_ref, bf16[2,704,256]{2,1,0:T(8,128)(2,1)} %get-tuple-element.58.refs_0_, bf16[2,704,256]{2,1,0:T(8,128)(2,1)} %get-tuple-element.59.refs_1_, bf16[2,704,256]{2,1,0:T(8,128)(2,1)} %copy-done.12, bf16[2,704,256]{2,1,0:T(8,128)(2,1)} %copy-done.13, ...), custom_call_target="tpu_custom_call" | custom-call | flops 2952790016 | bytes 11403264 | tf_op jit(solution)/shard_map/grad_x_own/pallas_call | solution.py:270
  281.9 4.7 %grad_down_own.1 = bf16[352,6144]{1,0:T(8,128)(2,1)} custom-call(s32[2]{0:T(128)} %pad_add_fusion.3.pick_ref, bf16[2,704,256]{2,1,0:T(8,128)(2,1)} %get-tuple-element.56.refs_0_, bf16[2,704,256]{2,1,0:T(8,128)(2,1)} %get-tuple-element.57.refs_1_, bf16[128,2048]{1,0:T(8,128)(2,1)} %copy-done.1, ...), custom_call_target="tpu_custom_call", output_to_operand_aliasing={{}: (9, {})} | custom-call | flops 738197504 | bytes 5341184 | tf_op jit(solution)/shard_map/grad_down_own/pallas_call | solution.py:270
  (159 shorter events, 81.8 us)
Async XLA Ops:
  2.0 15.2 %collective-permute-start.1 = (f32[4,128]{1,0:T(4,128)S(1)}, f32[4,128]{1,0:T(4,128)S(1)}, u32[]{:S(2)}, u32[]{:S(2)}) collective-permute-start(f32[4,128]{1,0:T(4,128)S(1)} %pad_maximum_fusion.meta_ref), channel_id=1, source_target_pairs={{0,8},{4,12},{8,24},{12,28},{16,0},{20,4},{24,16},{28,20},{1,9},{5... | collective-permute-start | bytes 6152 | tf_op jit(solution)/shard_map/ppermute | solution.py:315
  5.0 29.1 %collective-permute-start.2 = (bf16[128,2048]{1,0:T(8,128)(2,1)}, bf16[128,2048]{1,0:T(8,128)(2,1)S(1)}, u32[]{:S(2)}, u32[]{:S(2)}) collective-permute-start(bf16[128,2048]{1,0:T(8,128)(2,1)} %rows_ref.2), channel_id=1, source_target_pairs={{0,8},{4,12},{8,24},{12,28},{16,0},{20,4},{24,16},{28,20},{1,9},{5... | collective-permute-start | bytes 1572872 | tf_op jit(solution)/shard_map/ppermute | solution.py:315
  7.6 32.1 %collective-permute-start.5 = (bf16[128,2048]{1,0:T(8,128)(2,1)}, bf16[128,2048]{1,0:T(8,128)(2,1)S(1)}, u32[]{:S(2)}, u32[]{:S(2)}) collective-permute-start(bf16[128,2048]{1,0:T(8,128)(2,1)} %rows_ref.3), channel_id=1, source_target_pairs={{0,8},{4,12},{8,24},{12,28},{16,0},{20,4},{24,16},{28,20},{1,9},{5... | collective-permute-start | bytes 1572872 | tf_op jit(solution)/shard_map/ppermute | solution.py:315
  10.9 23.2 %collective-permute-start.4 = (bf16[64,2048]{1,0:T(8,128)(2,1)}, bf16[64,2048]{1,0:T(8,128)(2,1)S(1)}, u32[]{:S(2)}, u32[]{:S(2)}) collective-permute-start(bf16[64,2048]{1,0:T(8,128)(2,1)} %get-tuple-element.37), channel_id=1, source_target_pairs={{0,4},{4,0},{8,12},{12,8},{16,20},{20,16},{24,28},{28,24},{1,5},{5... | collective-permute-start | bytes 786440 | tf_op jit(solution)/shard_map/ppermute | solution.py:323
  14.7 17.8 %collective-permute-start = (bf16[64,2048]{1,0:T(8,128)(2,1)}, bf16[64,2048]{1,0:T(8,128)(2,1)S(1)}, u32[]{:S(2)}, u32[]{:S(2)}) collective-permute-start(bf16[64,2048]{1,0:T(8,128)(2,1)} %get-tuple-element.33), channel_id=1, source_target_pairs={{0,4},{4,0},{8,12},{12,8},{16,20},{20,16},{24,28},{28,24},{1,5},{5... | collective-permute-start | bytes 786440 | tf_op jit(solution)/shard_map/ppermute | solution.py:323
  17.2 13.6 %collective-permute-start.8 = (f32[4,128]{1,0:T(4,128)S(1)}, f32[4,128]{1,0:T(4,128)S(1)}, u32[]{:S(2)}, u32[]{:S(2)}) collective-permute-start(f32[4,128]{1,0:T(4,128)S(1)} %collective-permute-done.1.meta_ref), channel_id=1, source_target_pairs={{0,8},{4,12},{8,24},{12,28},{16,0},{20,4},{24,16},{28,20},{1,9},{5... | collective-permute-start | bytes 6152 | tf_op jit(solution)/shard_map/ppermute | solution.py:315
  30.8 56.5 %collective-permute-start.9 = (f32[4,128]{1,0:T(4,128)S(1)}, f32[4,128]{1,0:T(4,128)S(1)}, u32[]{:S(2)}, u32[]{:S(2)}) collective-permute-start(f32[4,128]{1,0:T(4,128)S(1)} %collective-permute-done.8.meta_ref), channel_id=1, source_target_pairs={{0,8},{4,12},{8,24},{12,28},{16,0},{20,4},{24,16},{28,20},{1,9},{5... | collective-permute-start | bytes 6152 | tf_op jit(solution)/shard_map/ppermute | solution.py:315
  32.5 112.1 %collective-permute-start.28 = (bf16[128,2048]{1,0:T(8,128)(2,1)S(1)}, bf16[128,2048]{1,0:T(8,128)(2,1)S(1)}, u32[]{:S(2)}, u32[]{:S(2)}) collective-permute-start(bf16[128,2048]{1,0:T(8,128)(2,1)S(1)} %constant_dynamic-update-slice_fusion.refs_0_.refs_4_), channel_id=1, source_target_pairs={{0,2},{1,3},{2,0},{3,1},{4,6},{5,7},{6,4},{7,5},{8,10},{9,11},{10,... | collective-permute-start | bytes 1572872 | tf_op jit(solution)/shard_map/ppermute | solution.py:326
  44.3 32.7 %collective-permute-start.10 = (bf16[128,2048]{1,0:T(8,128)(2,1)}, bf16[128,2048]{1,0:T(8,128)(2,1)S(1)}, u32[]{:S(2)}, u32[]{:S(2)}) collective-permute-start(bf16[128,2048]{1,0:T(8,128)(2,1)} %copy-done.21), channel_id=1, source_target_pairs={{0,8},{4,12},{8,24},{12,28},{16,0},{20,4},{24,16},{28,20},{1,9},{5... | collective-permute-start | bytes 1572872 | tf_op jit(solution)/shard_map/ppermute | solution.py:315
  45.8 25.7 %collective-permute-start.14 = (bf16[128,2048]{1,0:T(8,128)(2,1)}, bf16[128,2048]{1,0:T(8,128)(2,1)S(1)}, u32[]{:S(2)}, u32[]{:S(2)}) collective-permute-start(bf16[128,2048]{1,0:T(8,128)(2,1)} %copy-done.22), channel_id=1, source_target_pairs={{0,8},{4,12},{8,24},{12,28},{16,0},{20,4},{24,16},{28,20},{1,9},{5... | collective-permute-start | bytes 1572872 | tf_op jit(solution)/shard_map/ppermute | solution.py:315
  80.6 16.0 %collective-permute-start.12 = (bf16[128,2048]{1,0:T(8,128)(2,1)}, bf16[128,2048]{1,0:T(8,128)(2,1)S(1)}, u32[]{:S(2)}, u32[]{:S(2)}) collective-permute-start(bf16[128,2048]{1,0:T(8,128)(2,1)} %copy-done.24), channel_id=1, source_target_pairs={{0,8},{4,12},{8,24},{12,28},{16,0},{20,4},{24,16},{28,20},{1,9},{5... | collective-permute-start | bytes 1572872 | tf_op jit(solution)/shard_map/ppermute | solution.py:315
  83.0 21.3 %collective-permute-start.16 = (bf16[128,2048]{1,0:T(8,128)(2,1)}, bf16[128,2048]{1,0:T(8,128)(2,1)S(1)}, u32[]{:S(2)}, u32[]{:S(2)}) collective-permute-start(bf16[128,2048]{1,0:T(8,128)(2,1)} %copy-done.23), channel_id=1, source_target_pairs={{0,8},{4,12},{8,24},{12,28},{16,0},{20,4},{24,16},{28,20},{1,9},{5... | collective-permute-start | bytes 1572872 | tf_op jit(solution)/shard_map/ppermute | solution.py:315
  86.7 58.4 %collective-permute-start.29 = (bf16[128,2048]{1,0:T(8,128)(2,1)}, bf16[128,2048]{1,0:T(8,128)(2,1)S(1)}, u32[]{:S(2)}, u32[]{:S(2)}) collective-permute-start(bf16[128,2048]{1,0:T(8,128)(2,1)} %copy-done.7), channel_id=1, source_target_pairs={{0,2},{1,3},{2,0},{3,1},{4,6},{5,7},{6,4},{7,5},{8,10},{9,11},{10,... | collective-permute-start | bytes 1572872 | tf_op jit(solution)/shard_map/ppermute | solution.py:326
  142.5 81.1 %collective-permute-start.24 = (bf16[2,352,2048]{2,1,0:T(8,128)(2,1)}, bf16[2,352,2048]{2,1,0:T(8,128)(2,1)S(1)}, u32[]{:S(2)}, u32[]{:S(2)}) collective-permute-start(bf16[2,352,2048]{2,1,0:T(8,128)(2,1)} %grad_down_core.1), channel_id=1, source_target_pairs={{0,1},{1,0},{2,3},{3,2},{4,5},{5,4},{6,7},{7,6},{8,9},{9,8},{10,11... | collective-permute-start | bytes 8650760 | tf_op jit(solution)/shard_map/ppermute | solution.py:326
  142.5 19.2 %collective-permute-start.26 = (bf16[2,704,256]{2,1,0:T(8,128)(2,1)}, bf16[2,704,256]{2,1,0:T(8,128)(2,1)S(1)}, u32[]{:S(2)}, u32[]{:S(2)}) collective-permute-start(bf16[2,704,256]{2,1,0:T(8,128)(2,1)} %get-tuple-element.60), channel_id=1, source_target_pairs={{0,2},{1,3},{2,0},{3,1},{4,6},{5,7},{6,4},{7,5},{8,10},{9,11},{10,... | collective-permute-start | bytes 2162696 | tf_op jit(solution)/shard_map/ppermute | solution.py:326
  143.1 56.1 %collective-permute-start.27 = (bf16[2,704,256]{2,1,0:T(8,128)(2,1)}, bf16[2,704,256]{2,1,0:T(8,128)(2,1)S(1)}, u32[]{:S(2)}, u32[]{:S(2)}) collective-permute-start(bf16[2,704,256]{2,1,0:T(8,128)(2,1)} %get-tuple-element.61), channel_id=1, source_target_pairs={{0,2},{1,3},{2,0},{3,1},{4,6},{5,7},{6,4},{7,5},{8,10},{9,11},{10,... | collective-permute-start | bytes 2162696 | tf_op jit(solution)/shard_map/ppermute | solution.py:326
  144.6 43.8 %collective-permute-start.30 = (bf16[128,2048]{1,0:T(8,128)(2,1)S(1)}, bf16[128,2048]{1,0:T(8,128)(2,1)S(1)}, u32[]{:S(2)}, u32[]{:S(2)}) collective-permute-start(bf16[128,2048]{1,0:T(8,128)(2,1)S(1)} %copy-done.9), channel_id=1, source_target_pairs={{0,2},{1,3},{2,0},{3,1},{4,6},{5,7},{6,4},{7,5},{8,10},{9,11},{10,... | collective-permute-start | bytes 1572872 | tf_op jit(solution)/shard_map/ppermute | solution.py:326
  145.2 54.0 %collective-permute-start.31 = (bf16[128,2048]{1,0:T(8,128)(2,1)S(1)}, bf16[128,2048]{1,0:T(8,128)(2,1)S(1)}, u32[]{:S(2)}, u32[]{:S(2)}) collective-permute-start(bf16[128,2048]{1,0:T(8,128)(2,1)S(1)} %copy-done.11), channel_id=1, source_target_pairs={{0,2},{1,3},{2,0},{3,1},{4,6},{5,7},{6,4},{7,5},{8,10},{9,11},{10,... | collective-permute-start | bytes 1572872 | tf_op jit(solution)/shard_map/ppermute | solution.py:326
  209.0 62.8 %collective-permute-start.32 = (bf16[352,4096]{1,0:T(8,128)(2,1)}, bf16[352,4096]{1,0:T(8,128)(2,1)}, u32[]{:S(2)}, u32[]{:S(2)}) collective-permute-start(bf16[352,4096]{1,0:T(8,128)(2,1)} %grad_x_core.1), channel_id=1, source_target_pairs={{0,1},{1,0},{2,3},{3,2},{4,5},{5,4},{6,7},{7,6},{8,9},{9,8},{10,11... | collective-permute-start | bytes 8650760 | tf_op jit(solution)/shard_map/ppermute | solution.py:326
  220.8 14.6 %collective-permute-start.21 = (bf16[128,2048]{1,0:T(8,128)(2,1)}, bf16[128,2048]{1,0:T(8,128)(2,1)S(1)}, u32[]{:S(2)}, u32[]{:S(2)}) collective-permute-start(bf16[128,2048]{1,0:T(8,128)(2,1)} %merge.4), channel_id=1, source_target_pairs={{0,8},{4,12},{8,24},{12,28},{16,0},{20,4},{24,16},{28,20},{1,9},{5... | collective-permute-start | bytes 1572872 | tf_op jit(solution)/shard_map/ppermute | solution.py:315
  221.3 14.1 %collective-permute-start.19 = (bf16[64,2048]{1,0:T(8,128)(2,1)}, bf16[64,2048]{1,0:T(8,128)(2,1)S(1)}, u32[]{:S(2)}, u32[]{:S(2)}) collective-permute-start(bf16[64,2048]{1,0:T(8,128)(2,1)} %get-tuple-element.53), channel_id=1, source_target_pairs={{0,4},{4,0},{8,12},{12,8},{16,20},{20,16},{24,28},{28,24},{1,5},{5... | collective-permute-start | bytes 786440 | tf_op jit(solution)/shard_map/ppermute | solution.py:323
  229.6 51.2 %collective-permute-start.25 = (bf16[352,2048]{1,0:T(8,128)(2,1)}, bf16[352,2048]{1,0:T(8,128)(2,1)S(1)}, u32[]{:S(2)}, u32[]{:S(2)}) collective-permute-start(bf16[352,2048]{1,0:T(8,128)(2,1)} %grad_down_y.1), channel_id=1, source_target_pairs={{0,2},{1,3},{2,0},{3,1},{4,6},{5,7},{6,4},{7,5},{8,10},{9,11},{10,... | collective-permute-start | bytes 4325384 | tf_op jit(solution)/shard_map/ppermute | solution.py:326
  238.7 13.7 %collective-permute-start.22 = (bf16[128,2048]{1,0:T(8,128)(2,1)}, bf16[128,2048]{1,0:T(8,128)(2,1)S(1)}, u32[]{:S(2)}, u32[]{:S(2)}) collective-permute-start(bf16[128,2048]{1,0:T(8,128)(2,1)} %merge.5), channel_id=1, source_target_pairs={{0,8},{4,12},{8,24},{12,28},{16,0},{20,4},{24,16},{28,20},{1,9},{5... | collective-permute-start | bytes 1572872 | tf_op jit(solution)/shard_map/ppermute | solution.py:315
  255.7 12.8 %collective-permute-start.23 = (bf16[128,2048]{1,0:T(8,128)(2,1)}, bf16[128,2048]{1,0:T(8,128)(2,1)S(1)}, u32[]{:S(2)}, u32[]{:S(2)}) collective-permute-start(bf16[128,2048]{1,0:T(8,128)(2,1)} %merge.6), channel_id=1, source_target_pairs={{0,8},{4,12},{8,24},{12,28},{16,0},{20,4},{24,16},{28,20},{1,9},{5... | collective-permute-start | bytes 1572872 | tf_op jit(solution)/shard_map/ppermute | solution.py:315
  (47 other events, 492.6 us)

commit v2 on v0

v2 whole, which is shorter than its diff:
```python
import functools

import jax
import jax.numpy as jnp
from jax import lax
from jax.experimental import pallas as pl
from jax.experimental.pallas import tpu as pltpu
from jax.sharding import PartitionSpec as P

BF16 = jnp.bfloat16
F32 = jnp.float32
RING = (0, 1, 3, 2)
VMEM_LIMIT = 56 * 1024 * 1024


def params():
    return pltpu.CompilerParams(vmem_limit_bytes=VMEM_LIMIT)


def smem():
    return pl.BlockSpec(memory_space=pltpu.SMEM)


def small_cost():
    return pl.CostEstimate(flops=1024, bytes_accessed=1024, transcendentals=0)


def tile_of(width, most):
    return most if width % most == 0 else width


def placing_of(place_ref, meta_ref, column_count, capacity):
    tokens = meta_ref.shape[1]
    base, own = place_ref[0], place_ref[1]
    id_first, id_second = meta_ref[0:1, :], meta_ref[1:2, :]
    scale_first, scale_second = meta_ref[2:3, :], meta_ref[3:4, :]
    row = lax.broadcasted_iota(jnp.int32, (16, tokens), 0)
    expert = (base + jnp.bitwise_xor(row, own)).astype(F32)
    first = id_first == expert
    member = jnp.where(first | (id_second == expert), 1.0, 0.0)
    scale = jnp.where(first, scale_first, scale_second)
    earlier = lax.broadcasted_iota(jnp.int32, (tokens, tokens), 0)
    later = lax.broadcasted_iota(jnp.int32, (tokens, tokens), 1)
    before = jnp.where(earlier < later, 1.0, 0.0).astype(BF16)
    rank = jnp.dot(member.astype(BF16), before, preferred_element_type=F32)
    rank = jnp.where(member > 0.0, rank, -1.0)
    slot = lax.broadcasted_iota(jnp.int32, (capacity, tokens), 0).astype(F32)
    hits, scales = [], []
    for d in range(column_count):
        hit = jnp.where(rank[d : d + 1, :] == slot, 1.0, 0.0)
        hits.append(hit)
        scales.append(jnp.sum(hit * scale[d : d + 1, :], axis=1, keepdims=True))
    return jnp.concatenate(hits, axis=0), jnp.concatenate(scales, axis=0)


def select_kernel(column_count, capacity, place_ref, meta_ref, x_ref, d_ref, *refs):
    out_refs, (hits_ref, hits_all, scales_all) = refs[:column_count], refs[column_count:]

    @pl.when(pl.program_id(0) == 0)
    def _():
        hits, scales = placing_of(place_ref, meta_ref, column_count, capacity)
        hits_all[...] = hits.astype(BF16)
        hits_ref[...] = hits.astype(BF16)
        scales_all[...] = jnp.broadcast_to(scales, scales_all.shape)

    hits = hits_all[...]
    x = jnp.dot(hits, x_ref[...], preferred_element_type=F32).astype(BF16)
    dy = jnp.dot(hits, d_ref[...], preferred_element_type=F32)
    dy = (dy * scales_all[:, 0:1]).astype(BF16)
    for d in range(column_count):
        out_refs[d][0] = x[d * capacity : (d + 1) * capacity, :]
        out_refs[d][1] = dy[d * capacity : (d + 1) * capacity, :]


def select(place, meta, x, d_rows, column_count, capacity):
    tokens, width = x.shape
    tile = tile_of(width, 512)
    slot_count = column_count * capacity
    block = pl.BlockSpec((tokens, tile), lambda n: (0, n))
    outs = pl.pallas_call(
        functools.partial(select_kernel, column_count, capacity),
        grid=(width // tile,),
        out_shape=[jax.ShapeDtypeStruct((2, capacity, width), BF16)] * column_count
        + [jax.ShapeDtypeStruct((slot_count, tokens), BF16)],
        in_specs=[smem(), pl.BlockSpec(meta.shape, lambda n: (0, 0)), block, block],
        out_specs=[pl.BlockSpec((2, capacity, tile), lambda n: (0, 0, n))] * column_count
        + [pl.BlockSpec((slot_count, tokens), lambda n: (0, 0))],
        scratch_shapes=[
            pltpu.VMEM((slot_count, tokens), BF16),
            pltpu.VMEM((slot_count, 128), F32),
        ],
        compiler_params=params(),
        cost_estimate=small_cost(),
        name="select",
    )(place, meta, x, d_rows)
    return outs[:-1], outs[-1]


def merge_kernel(column_count, has_carry, hits_ref, *refs):
    slots = jnp.concatenate([part[...] for part in refs[:column_count]], axis=0)
    total = lax.dot_general(
        hits_ref[...], slots, (((0,), (0,)), ((), ())), preferred_element_type=F32
    )
    if has_carry:
        total = total + refs[column_count][...].astype(F32)
    refs[-1][...] = total.astype(BF16)


def merge(hits, parts, carry):
    column_count, (capacity, width) = len(parts), parts[0].shape
    tokens = hits.shape[1]
    tile = tile_of(width, 512)
    rows_block = pl.BlockSpec((tokens, tile), lambda n: (0, n))
    carries = [] if carry is None else [carry]
    return pl.pallas_call(
        functools.partial(merge_kernel, column_count, carry is not None),
        grid=(width // tile,),
        out_shape=jax.ShapeDtypeStruct((tokens, width), BF16),
        in_specs=[pl.BlockSpec(hits.shape, lambda n: (0, 0))]
        + [pl.BlockSpec((capacity, tile), lambda n: (0, n))] * column_count
        + [rows_block] * len(carries),
        out_specs=rows_block,
        compiler_params=params(),
        cost_estimate=small_cost(),
        name="merge",
    )(hits, *parts, *carries)


def expert_kernel(piece_count, capacity, place_ref, *refs):
    slot_refs, refs = refs[:piece_count], refs[piece_count:]
    w_ref, send_ref, keep_ref, hid_ref = refs[:4]
    dx_refs, refs = refs[4 : 4 + piece_count], refs[4 + piece_count :]
    x_all, dy_all, x_turned, dy_turned, w_pair, w_down, turned, slot_sems, w_sems = refs
    part, width = w_down.shape[1:]
    high = place_ref[2]

    slot_copies = []
    for i, ref in enumerate(slot_refs):
        rows = pl.ds(i * capacity, capacity)
        for k, target in enumerate((x_all, dy_all)):
            slot_copies.append(
                pltpu.make_async_copy(ref.at[k], target.at[rows], slot_sems.at[2 * i + k])
            )
    w_copies = []
    for t in range(2):
        rows = pl.ds(pl.multiple_of(jnp.bitwise_xor(high, 1 - t) * part, part), part)
        targets = (
            w_pair.at[pl.ds(2 * t * part, part)],
            w_pair.at[pl.ds((2 * t + 1) * part, part)],
            w_down.at[t],
        )
        for k, target in enumerate(targets):
            source = w_ref.at[0, rows, pl.ds(k * width, width)]
            w_copies.append(pltpu.make_async_copy(source, target, w_sems.at[3 * t + k]))
    for copy in slot_copies + w_copies:
        copy.start()
    for copy in slot_copies:
        copy.wait()
    x_turned[...] = x_all[...].T
    dy_turned[...] = dy_all[...].T
    for t in range(2):
        w_copies[3 * t].wait()
        w_copies[3 * t + 1].wait()
        both = jnp.dot(
            w_pair[2 * t * part : (2 * t + 2) * part, :],
            x_turned[...],
            preferred_element_type=F32,
        )
        w_copies[3 * t + 2].wait()
        d_hidden = jnp.dot(w_down[t], dy_turned[...], preferred_element_type=F32)
        gate, up = both[:part], both[part:]
        sig = jax.nn.sigmoid(gate)
        act = gate * sig
        d_up = (d_hidden * act).astype(BF16)
        d_gate = (d_hidden * up * sig * (1.0 + gate * (1.0 - sig))).astype(BF16)
        hid_ref[jnp.bitwise_xor(high, 1 - t)] = (act * up).astype(BF16)
        out_ref = (send_ref, keep_ref)[t]
        out_ref[:part, :] = d_gate
        out_ref[part:, :] = d_up
        turned[:, 2 * t * part : (2 * t + 1) * part] = d_gate.T
        turned[:, (2 * t + 1) * part : (2 * t + 2) * part] = d_up.T
    total = jnp.dot(turned[...], w_pair[...], preferred_element_type=F32).astype(BF16)
    for i in range(piece_count):
        dx_refs[i][...] = total[i * capacity : (i + 1) * capacity, :]


def expert(place, slots, w_stack):
    piece_count = len(slots)
    _, capacity, width = slots[0].shape
    rows = piece_count * capacity
    hidden = w_stack.shape[1]
    part = hidden // 2
    anywhere = pl.BlockSpec(memory_space=pl.ANY)
    inside = pl.BlockSpec(memory_space=pltpu.VMEM)
    outs = pl.pallas_call(
        functools.partial(expert_kernel, piece_count, capacity),
        in_specs=[smem()] + [anywhere] * (piece_count + 1),
        out_specs=[inside] * (3 + piece_count),
        out_shape=[
            jax.ShapeDtypeStruct((hidden, rows), BF16),
            jax.ShapeDtypeStruct((hidden, rows), BF16),
            jax.ShapeDtypeStruct((2, part, rows), BF16),
        ]
        + [jax.ShapeDtypeStruct((capacity, width), BF16)] * piece_count,
        scratch_shapes=[
            pltpu.VMEM((rows, width), BF16),
            pltpu.VMEM((rows, width), BF16),
            pltpu.VMEM((width, rows), BF16),
            pltpu.VMEM((width, rows), BF16),
            pltpu.VMEM((2 * hidden, width), BF16),
            pltpu.VMEM((2, part, width), BF16),
            pltpu.VMEM((rows, 2 * hidden), BF16),
            pltpu.SemaphoreType.DMA((2 * piece_count,)),
            pltpu.SemaphoreType.DMA((6,)),
        ],
        compiler_params=params(),
        cost_estimate=small_cost(),
        name="expert",
    )(place, *slots, w_stack)
    return outs[0], outs[1], outs[2], outs[3:]


def grad_x_kernel(act_count, place_ref, *refs):
    acts, rows = refs[:act_count], refs[act_count:-2]
    send_ref, keep_ref = refs[-2:]
    own = send_ref.shape[1]
    low = place_ref[3]
    right = jnp.concatenate(
        [ref[0] if len(ref.shape) == 3 else ref[...] for ref in rows], axis=0
    )
    lefts = []
    for who in (1 - low, low):
        for lead in range(2):
            start = pl.multiple_of((2 * lead + who) * own, own)
            lefts.append(jnp.concatenate([ref[pl.ds(start, own), :] for ref in acts], axis=1))
    total = jnp.dot(jnp.concatenate(lefts, axis=0), right, preferred_element_type=F32).astype(BF16)
    send_ref[0] = total[:own]
    send_ref[1] = total[own : 2 * own]
    keep_ref[0] = total[2 * own : 3 * own]
    keep_ref[1] = total[3 * own :]


def rows_spec(array, tile, lead):
    if array.ndim == 3:
        return pl.BlockSpec((1, array.shape[1], tile), lambda n: (lead, 0, n))
    return pl.BlockSpec((array.shape[0], tile), lambda n: (0, n))


def grad_x(place, acts, rows):
    own = acts[0].shape[0] // 4
    width = rows[0].shape[-1]
    tile = tile_of(width, 512)
    out_spec = pl.BlockSpec((2, own, tile), lambda n: (0, 0, n))
    return pl.pallas_call(
        functools.partial(grad_x_kernel, len(acts)),
        grid=(width // tile,),
        in_specs=[smem()]
        + [pl.BlockSpec(act.shape, lambda n: (0, 0)) for act in acts]
        + [rows_spec(row, tile, 0) for row in rows],
        out_specs=[out_spec, out_spec],
        out_shape=[jax.ShapeDtypeStruct((2, own, width), BF16)] * 2,
        compiler_params=params(),
        cost_estimate=small_cost(),
        name="grad_x",
    )(place, *acts, *rows)


def grad_down_kernel(act_count, other, place_ref, *refs):
    acts, rows = refs[:act_count], refs[act_count:-2]
    send_ref, keep_ref = refs[-2:]
    own = send_ref.shape[0]
    high, low = place_ref[2], place_ref[3]
    lead = 1 - high if other else high
    right = jnp.concatenate([ref[0] for ref in rows], axis=0)
    lefts = []
    for who in (1 - low, low):
        start = pl.multiple_of(who * own, own)
        lefts.append(jnp.concatenate([ref[lead, pl.ds(start, own), :] for ref in acts], axis=1))
    total = jnp.dot(jnp.concatenate(lefts, axis=0), right, preferred_element_type=F32).astype(BF16)
    send_ref[...] = total[:own]
    keep_ref[...] = total[own:]


def grad_down(place, acts, rows, other):
    own = acts[0].shape[1] // 2
    width = rows[0].shape[-1]
    tile = tile_of(width, 512)
    out_spec = pl.BlockSpec((own, tile), lambda n: (0, n))
    return pl.pallas_call(
        functools.partial(grad_down_kernel, len(acts), other),
        grid=(width // tile,),
        in_specs=[smem()]
        + [pl.BlockSpec(act.shape, lambda n: (0, 0, 0)) for act in acts]
        + [rows_spec(row, tile, 1) for row in rows],
        out_specs=[out_spec, out_spec],
        out_shape=[jax.ShapeDtypeStruct((own, width), BF16)] * 2,
        compiler_params=params(),
        cost_estimate=small_cost(),
        name="grad_down_other" if other else "grad_down_own",
    )(place, *acts, *rows)


def add_kernel(term_count, *refs):
    total = refs[0][...].astype(F32)
    for ref in refs[1:term_count]:
        total = total + ref[...].astype(F32)
    out_ref = refs[-1]
    out_ref[...] = total.astype(BF16).reshape(out_ref.shape)


def add_into(terms, columns, first, into, name):
    leads, own, width = terms[0].shape
    tile = tile_of(width, 1024)
    tiles = width // tile
    aliases, operands = {}, list(terms)
    in_specs = [pl.BlockSpec((1, own, tile), lambda i, n: (i, 0, n))] * len(terms)
    if into is not None:
        aliases = {len(operands): 0}
        operands.append(into)
        in_specs.append(pl.BlockSpec(memory_space=pl.ANY))
    return pl.pallas_call(
        functools.partial(add_kernel, len(terms)),
        grid=(leads, tiles),
        in_specs=in_specs,
        out_specs=pl.BlockSpec((own, tile), lambda i, n: (0, first // tile + i * tiles + n)),
        out_shape=jax.ShapeDtypeStruct((own, columns), BF16),
        input_output_aliases=aliases,
        compiler_params=params(),
        cost_estimate=small_cost(),
        name=name,
    )(*operands)


def body(x_tokens, d_out, expert_ids, combine, w_stack):
    tokens, width = x_tokens.shape
    experts = lax.axis_size("expert")
    replicas = lax.axis_size("replica")
    plane_count = len(RING)
    columns = experts // plane_count
    capacity = 2 * tokens * expert_ids.shape[1] // experts

    position = lax.axis_index("expert")
    replica = lax.axis_index("replica")
    plane, column = position // columns, position % columns
    high, low = replica // 2, replica % 2
    place = jnp.stack([plane * columns, column, high, low]).astype(jnp.int32)

    def along_ring(value, hops=1):
        pairs = [
            (RING[i] * columns + c, RING[(i + hops) % plane_count] * columns + c)
            for i in range(plane_count)
            for c in range(columns)
        ]
        return lax.ppermute(value, "expert", pairs)

    def across_columns(value, d):
        pairs = [
            (p * columns + c, p * columns + (c ^ d))
            for p in range(plane_count)
            for c in range(columns)
        ]
        return lax.ppermute(value, "expert", pairs)

    def across_replicas(value, d):
        return lax.ppermute(value, "replica", [(r, r ^ d) for r in range(replicas)])

    meta = jnp.concatenate([expert_ids.T.astype(F32), combine.T], axis=0)
    metas, x_blocks, d_blocks = [meta], [x_tokens], [d_out]
    for s in range(1, plane_count):
        metas.append(along_ring(meta, s))
        x_blocks.append(along_ring(x_blocks[-1]))
        d_blocks.append(along_ring(d_blocks[-1]))

    slots, hits, x_other = [], [], []
    for s in range(plane_count):
        picked, hit = select(place, metas[s], x_blocks[s], d_blocks[s], columns, capacity)
        arrived = [picked[0]] + [across_columns(picked[d], d) for d in range(1, columns)]
        slots.append(arrived)
        hits.append(hit)
        x_other.append(
            across_replicas(jnp.concatenate([piece[0] for piece in arrived], axis=0), 2)
        )

    keeps, arrivals, hids, pieces = [], [], [], []
    group = 2
    for g in range(0, plane_count, group):
        group_slots = [piece for s in range(g, g + group) for piece in slots[s]]
        send, keep, hid, dx = expert(place, group_slots, w_stack)
        keeps.append(keep)
        arrivals.append(across_replicas(send, 2))
        hids.append(hid)
        pieces.extend(dx)

    def dx_parts(s):
        mine = pieces[s * columns : (s + 1) * columns]
        return [mine[0]] + [across_columns(mine[d], d) for d in range(1, columns)]

    carry = None
    for s in range(1, plane_count):
        carry = along_ring(merge(hits[s], dx_parts(s), carry))
    d_tokens = merge(hits[0], dx_parts(0), carry)

    all_slots = [piece for arrived in slots for piece in arrived]
    send, keep = grad_down(place, hids, all_slots, True)
    across = keep.astype(F32) + across_replicas(send, 1).astype(F32)
    down_y = across_replicas(across.astype(BF16), 2)
    send, down_own = grad_down(place, hids, all_slots, False)
    down_core = across_replicas(send, 1)
    send, keep = grad_x(place, keeps + arrivals, all_slots + x_other)
    g_rows = add_into([keep, across_replicas(send, 1)], 3 * width, 0, None, "sum_x")
    down_terms = [term[None] for term in (down_own, down_core, down_y)]
    g_rows = add_into(down_terms, 3 * width, 2 * width, g_rows, "sum_down")
    return d_tokens, g_rows[None]


def solution(mesh):
    return jax.shard_map(
        body,
        mesh=mesh,
        in_specs=(
            P(("expert", "replica"), None),
            P(("expert", "replica"), None),
            P(("expert", "replica"), None),
            P(("expert", "replica"), None),
            P("expert", None, None),
        ),
        out_specs=(P(("expert", "replica"), None), P("expert", "replica", None)),
        check_vma=False,
    )
```

time: 286 us -> 267 us (0.934)
  Pallas kernels: 0 us -> 103 us
  matrix products: 58.9 us -> 0 us
  waiting for transfers between devices: 165 us -> 110 us
  starting transfers between devices: 15.3 us -> 32.7 us
  between operations: 14.3 us -> 1.01 us
  other arithmetic: 15.9 us -> 3.83 us
    all_to_all x3 -> x0, waiting for transfers between devices: 119 us -> none  [the longest x1 46.9 us: body(): lax.all_to_all(dx_slots.astype(jnp.bfloat16), 'expert', split_axis=0, con...]
    ppermute x0 -> x30, waiting for transfers between devices: none -> 110 us  [the longest x12 52.8 us: along_ring(): return lax.ppermute(value, 'expert', pairs)]
    pallas_call x0 -> x15, Pallas kernels: none -> 103 us  [the longest x2 42.1 us: expert(): pl.pallas_call(functools.partial(expert_kernel, piece_count, capacity), i...]
    dot_general x10 -> x0, matrix products: 58.9 us -> none  [the longest x3 13.4 us: contract_rows(): lax.dot_general(factor, operand, (((0,), (0,)), ((), ())), preferred_elem...]
    reduce_scatter x1 -> x0, waiting for transfers between devices: 45.7 us -> none  [body(): lax.psum_scatter(jnp.concatenate([part_term(gate_rows, x_rows), part_term...]
    ppermute x0 -> x30, starting transfers between devices: none -> 32.7 us  [the longest x12 14 us: along_ring(): return lax.ppermute(value, 'expert', pairs)]
    all_to_all x3 -> x0, starting transfers between devices: 15.1 us -> none  [the longest x1 7.38 us: body(): lax.all_to_all(send_x, 'expert', split_axis=0, concat_axis=0, tiled=True)]
    unnamed x20 -> x74, local copies, waits for them, and re-layouts: 2.27 us -> 11.8 us
  transfers between devices with their start and end apart: 4 -> 30, of which waited for: 4 -> 13; matrix products, arithmetic and copies ran while one was open for 19% -> 2% of each run, Pallas kernels for 0% -> 38%
where the time goes in v2:
time: 267 us; the launch traced here: 266 us
  waiting for transfers between devices  110 us (41%)
  Pallas kernels  103 us (39%)
  starting transfers between devices  32.7 us (12%)
  local copies, waits for them, and re-layouts  14.8 us (6%)
  other arithmetic  3.83 us (1%)
    ppermute x12, waiting for transfers between devices, along_ring(): return lax.ppermute(value, 'expert', pairs)  52.8 us
    pallas_call x2, Pallas kernels, expert(): pl.pallas_call(functools.partial(expert_kernel, piece_count, capacity), i...  42.1 us
    ppermute x8, waiting for transfers between devices, across_columns(): return lax.ppermute(value, 'expert', pairs)  30 us
    ppermute x10, waiting for transfers between devices, across_replicas(): return lax.ppermute(value, 'replica', [(r, r ^ d) for r in range(replicas)])  27.5 us
    pallas_call x4, Pallas kernels, select(): pl.pallas_call(functools.partial(select_kernel, column_count, capacity),...  16.6 us
    pallas_call x4, Pallas kernels, merge(): pl.pallas_call(functools.partial(merge_kernel, column_count, carry is not...  14.8 us
    ppermute x12, starting transfers between devices, along_ring(): return lax.ppermute(value, 'expert', pairs)  14 us
    unnamed x74, local copies, waits for them, and re-layouts  11.8 us
  transfers between devices with their start and end apart: 30, of which 13 were waited for; matrix products, arithmetic and copies ran while one was open for 2% of the time, Pallas kernels for 38%

profile of v2, /device:TPU:0, one launch (start us, length us, event | category | flops | bytes accessed | tf_op | source)
XLA Modules:
  0.0 265.7 jit_solution(2694195914972323750)
XLA Ops:
  2.0 5.0 %collective-permute-start.11 = (f32[4,128]{1,0:T(4,128)S(1)}, f32[4,128]{1,0:T(4,128)S(1)}, u32[]{:S(2)}, u32[]{:S(2)}) collective-permute-start(f32[4,128]{1,0:T(4,128)S(1)} %pad_maximum_fusion.4.meta_ref), channel_id=1, source_target_pairs={{0,24},{4,28},{8,16},{12,20},{24,0},{28,4},{16,8},{20,12},{1,25},{... | collective-permute-start | bytes 6152 | tf_op jit(solution)/shard_map/ppermute | solution.py:354
  9.1 4.1 %select.16 = (bf16[2,64,2048]{2,1,0:T(8,128)(2,1)}, bf16[2,64,2048]{2,1,0:T(8,128)(2,1)}, bf16[128,128]{1,0:T(8,128)(2,1)}) custom-call(s32[4]{0:T(128)} %pad_add_fusion.place_ref, f32[4,128]{1,0:T(4,128)} %copy-done.29, bf16[128,2048]{1,0:T(8,128)(2,1)} %x_ref.1, bf16[128,2048]{1,0:T(8,128)(2,1)} %d_ref.1), custom_call_target="tpu_custom_call" | custom-call | flops 1024 | bytes 1024 | tf_op jit(solution)/shard_map/select/pallas_call | solution.py:80
  15.7 17.2 %collective-permute-done.1.meta_ref = f32[4,128]{1,0:T(4,128)S(1)} collective-permute-done((f32[4,128]{1,0:T(4,128)S(1)}, f32[4,128]{1,0:T(4,128)S(1)}, u32[]{:S(2)}, u32[]{:S(2)}) %collective-permute-start.1) | collective-permute-done | bytes 2080 | tf_op jit(solution)/shard_map/ppermute | solution.py:354
  34.5 4.2 %select.17 = (bf16[2,64,2048]{2,1,0:T(8,128)(2,1)}, bf16[2,64,2048]{2,1,0:T(8,128)(2,1)}, bf16[128,128]{1,0:T(8,128)(2,1)}) custom-call(s32[4]{0:T(128)} %pad_add_fusion.place_ref, f32[4,128]{1,0:T(4,128)} %copy-done.32, bf16[128,2048]{1,0:T(8,128)(2,1)} %copy-done.19, bf16[128,2048]{1,0:T(8,128)(2,1)} %copy-done.20), custom_call_target="tpu_custom_call" | custom-call | flops 1024 | bytes 1024 | tf_op jit(solution)/shard_map/select/pallas_call | solution.py:80
  45.2 10.9 %collective-permute-done.7.x_ref = bf16[128,2048]{1,0:T(8,128)(2,1)S(1)} collective-permute-done((bf16[128,2048]{1,0:T(8,128)(2,1)}, bf16[128,2048]{1,0:T(8,128)(2,1)S(1)}, u32[]{:S(2)}, u32[]{:S(2)}) %collective-permute-start.7) | collective-permute-done | bytes 524320 | tf_op jit(solution)/shard_map/ppermute | solution.py:354
  56.1 8.6 %collective-permute-done.9.d_ref = bf16[128,2048]{1,0:T(8,128)(2,1)S(1)} collective-permute-done((bf16[128,2048]{1,0:T(8,128)(2,1)}, bf16[128,2048]{1,0:T(8,128)(2,1)S(1)}, u32[]{:S(2)}, u32[]{:S(2)}) %collective-permute-start.9) | collective-permute-done | bytes 524320 | tf_op jit(solution)/shard_map/ppermute | solution.py:354
  65.6 4.1 %select.19 = (bf16[2,64,2048]{2,1,0:T(8,128)(2,1)}, bf16[2,64,2048]{2,1,0:T(8,128)(2,1)}, bf16[128,128]{1,0:T(8,128)(2,1)}) custom-call(s32[4]{0:T(128)} %pad_add_fusion.place_ref, f32[4,128]{1,0:T(4,128)} %copy-done.30, bf16[128,2048]{1,0:T(8,128)(2,1)} %copy-done.21, bf16[128,2048]{1,0:T(8,128)(2,1)} %copy-done.22), custom_call_target="tpu_custom_call" | custom-call | flops 1024 | bytes 1024 | tf_op jit(solution)/shard_map/select/pallas_call | solution.py:80
  73.7 21.0 %expert.2 = (bf16[1408,256]{1,0:T(8,128)(2,1)}, bf16[1408,256]{1,0:T(8,128)(2,1)}, bf16[2,704,256]{2,1,0:T(8,128)(2,1)}, bf16[64,2048]{1,0:T(8,128)(2,1)}, bf16[...) custom-call(s32[4]{0:T(128)} %pad_add_fusion.place_ref, ...), custom_call_target="tpu_custom_call" | custom-call | flops 1024 | bytes 1024 | tf_op jit(solution)/shard_map/expert/pallas_call | solution.py:195
  98.0 4.2 %select.18 = (bf16[2,64,2048]{2,1,0:T(8,128)(2,1)}, bf16[2,64,2048]{2,1,0:T(8,128)(2,1)}, bf16[128,128]{1,0:T(8,128)(2,1)}) custom-call(s32[4]{0:T(128)} %pad_add_fusion.place_ref, f32[4,128]{1,0:T(4,128)} %copy-done.31, bf16[128,2048]{1,0:T(8,128)(2,1)} %copy-done.23, bf16[128,2048]{1,0:T(8,128)(2,1)} %copy-done.24), custom_call_target="tpu_custom_call" | custom-call | flops 1024 | bytes 1024 | tf_op jit(solution)/shard_map/select/pallas_call | solution.py:80
  103.8 8.8 %collective-permute-done.13.refs_3_.refs_9_.refs_11_ = bf16[2,64,2048]{2,1,0:T(8,128)(2,1)S(1)} collective-permute-done((bf16[2,64,2048]{2,1,0:T(8,128)(2,1)}, bf16[2,64,2048]{2,1,0:T(8,128)(2,1)S(1)}, u32[]{:S(2)}, u32[]{:S(2)}) %collective-permute-start.13) | collective-permute-done | bytes 524320 | tf_op jit(solution)/shard_map/ppermute | solution.py:362
  113.5 21.1 %expert.3 = (bf16[1408,256]{1,0:T(8,128)(2,1)}, bf16[1408,256]{1,0:T(8,128)(2,1)}, bf16[2,704,256]{2,1,0:T(8,128)(2,1)}, bf16[64,2048]{1,0:T(8,128)(2,1)}, bf16[...) custom-call(s32[4]{0:T(128)} %pad_add_fusion.place_ref, ...), custom_call_target="tpu_custom_call" | custom-call | flops 1024 | bytes 1024 | tf_op jit(solution)/shard_map/expert/pallas_call | solution.py:195
  135.5 5.5 %grad_down_other.1 = (bf16[352,2048]{1,0:T(8,128)(2,1)}, bf16[352,2048]{1,0:T(8,128)(2,1)}) custom-call(s32[4]{0:T(128)} %pad_add_fusion.place_ref, bf16[2,704,256]{2,1,0:T(8,128)(2,1)} %get-tuple-element.54.refs_0_, bf16[2,704,256]{2,1,0:T(8,128)(2,1)} %get-tuple-element.55.refs_1_, bf16[2,64,2048]{2,1,0:T(8,128)(2,1)} %get-tuple-element.35.refs_0_.refs_2_.refs_4_, ...), custom_call_target="tpu_custom_call" | custom-call | flops 1024 | bytes 1024 | tf_op jit(solution)/shard_map/grad_down_other/pallas_call | solution.py:289
  143.3 20.1 %collective-permute-done.27.refs_14_ = bf16[128,2048]{1,0:T(8,128)(2,1)S(1)} collective-permute-done((bf16[128,2048]{1,0:T(8,128)(2,1)S(1)}, bf16[128,2048]{1,0:T(8,128)(2,1)S(1)}, u32[]{:S(2)}, u32[]{:S(2)}) %collective-permute-start.27) | collective-permute-done | bytes 524320 | tf_op jit(solution)/shard_map/ppermute | solution.py:365
  163.5 7.3 %collective-permute-done.28.refs_15_ = bf16[128,2048]{1,0:T(8,128)(2,1)S(1)} collective-permute-done((bf16[128,2048]{1,0:T(8,128)(2,1)S(1)}, bf16[128,2048]{1,0:T(8,128)(2,1)S(1)}, u32[]{:S(2)}, u32[]{:S(2)}) %collective-permute-start.28) | collective-permute-done | bytes 524320 | tf_op jit(solution)/shard_map/ppermute | solution.py:365
  171.9 10.2 %grad_x.1 = (bf16[2,352,2048]{2,1,0:T(8,128)(2,1)}, bf16[2,352,2048]{2,1,0:T(8,128)(2,1)}) custom-call(s32[4]{0:T(128)} %pad_add_fusion.place_ref, bf16[1408,256]{1,0:T(8,128)(2,1)} %get-tuple-element.60.refs_0_, bf16[1408,256]{1,0:T(8,128)(2,1)} %get-tuple-element.61.refs_1_, bf16[1408,256]{1,0:T(8,128)(2,1)} %copy-done.10, bf16[1408,256]{1,0:T(8,128)(2,1)} %copy-done.11, ...), custom_call_target="tpu_custom_call" | custom-call | flops 1024 | bytes 1024 | tf_op jit(solution)/shard_map/grad_x/pallas_call | solution.py:254
  183.8 7.2 %collective-permute-done.16.refs_1_ = bf16[64,2048]{1,0:T(8,128)(2,1)S(1)} collective-permute-done((bf16[64,2048]{1,0:T(8,128)(2,1)S(1)}, bf16[64,2048]{1,0:T(8,128)(2,1)S(1)}, u32[]{:S(2)}, u32[]{:S(2)}) %collective-permute-start.16) | collective-permute-done | bytes 262176 | tf_op jit(solution)/shard_map/ppermute | solution.py:362
  196.4 5.7 %grad_down_own.1 = (bf16[352,2048]{1,0:T(8,128)(2,1)}, bf16[352,2048]{1,0:T(8,128)(2,1)}) custom-call(s32[4]{0:T(128)} %pad_add_fusion.place_ref, bf16[2,704,256]{2,1,0:T(8,128)(2,1)} %get-tuple-element.54.refs_0_, bf16[2,704,256]{2,1,0:T(8,128)(2,1)} %get-tuple-element.55.refs_1_, bf16[2,64,2048]{2,1,0:T(8,128)(2,1)} %get-tuple-element.35.refs_0_.refs_2_.refs_4_, ...), custom_call_target="tpu_custom_call" | custom-call | flops 1024 | bytes 1024 | tf_op jit(solution)/shard_map/grad_down_own/pallas_call | solution.py:289
  213.7 3.8 %merge.5 = bf16[128,2048]{1,0:T(8,128)(2,1)} custom-call(bf16[128,128]{1,0:T(8,128)(2,1)} %get-tuple-element.48.hits_ref, bf16[64,2048]{1,0:T(8,128)(2,1)} %get-tuple-element.49.refs_0_, bf16[64,2048]{1,0:T(8,128)(2,1)} %copy-done.27, bf16[128,2048]{1,0:T(8,128)(2,1)} %copy-done.14), custom_call_target="tpu_custom_call" | custom-call | flops 1024 | bytes 1024 | tf_op jit(solution)/shard_map/merge/pallas_call | solution.py:115
  220.2 5.8 %collective-permute-done.14.refs_1_ = bf16[64,2048]{1,0:T(8,128)(2,1)S(1)} collective-permute-done((bf16[64,2048]{1,0:T(8,128)(2,1)S(1)}, bf16[64,2048]{1,0:T(8,128)(2,1)S(1)}, u32[]{:S(2)}, u32[]{:S(2)}) %collective-permute-start.14) | collective-permute-done | bytes 262176 | tf_op jit(solution)/shard_map/ppermute | solution.py:362
  226.0 5.8 %collective-permute-done.18.refs_2_ = bf16[128,2048]{1,0:T(8,128)(2,1)S(1)} collective-permute-done((bf16[128,2048]{1,0:T(8,128)(2,1)}, bf16[128,2048]{1,0:T(8,128)(2,1)S(1)}, u32[]{:S(2)}, u32[]{:S(2)}) %collective-permute-start.18) | collective-permute-done | bytes 524320 | tf_op jit(solution)/shard_map/ppermute | solution.py:354
  232.6 3.8 %merge.6 = bf16[128,2048]{1,0:T(8,128)(2,1)} custom-call(bf16[128,128]{1,0:T(8,128)(2,1)} %get-tuple-element.41.hits_ref, bf16[64,2048]{1,0:T(8,128)(2,1)} %get-tuple-element.46.refs_0_, bf16[64,2048]{1,0:T(8,128)(2,1)} %copy-done.25, bf16[128,2048]{1,0:T(8,128)(2,1)} %copy-done.17), custom_call_target="tpu_custom_call" | custom-call | flops 1024 | bytes 1024 | tf_op jit(solution)/shard_map/merge/pallas_call | solution.py:115
  238.1 5.0 %collective-permute-done.5.refs_1_ = bf16[64,2048]{1,0:T(8,128)(2,1)S(1)} collective-permute-done((bf16[64,2048]{1,0:T(8,128)(2,1)S(1)}, bf16[64,2048]{1,0:T(8,128)(2,1)S(1)}, u32[]{:S(2)}, u32[]{:S(2)}) %collective-permute-start.5) | collective-permute-done | bytes 262176 | tf_op jit(solution)/shard_map/ppermute | solution.py:362
  243.1 6.7 %collective-permute-done.19.refs_2_ = bf16[128,2048]{1,0:T(8,128)(2,1)S(1)} collective-permute-done((bf16[128,2048]{1,0:T(8,128)(2,1)}, bf16[128,2048]{1,0:T(8,128)(2,1)S(1)}, u32[]{:S(2)}, u32[]{:S(2)}) %collective-permute-start.19) | collective-permute-done | bytes 524320 | tf_op jit(solution)/shard_map/ppermute | solution.py:354
  255.9 4.9 %sum_x.1.refs_3_ = bf16[352,6144]{1,0:T(8,128)(2,1)} custom-call(bf16[2,352,2048]{2,1,0:T(8,128)(2,1)} %get-tuple-element.64.refs_0_, bf16[2,352,2048]{2,1,0:T(8,128)(2,1)} %copy-done.6), custom_call_target="tpu_custom_call" | custom-call | flops 1024 | bytes 1024 | tf_op jit(solution)/shard_map/sum_x/pallas_call | solution.py:321
  (141 shorter events, 63.7 us)
Async XLA Ops:
  2.0 41.6 %collective-permute-start.11 = (f32[4,128]{1,0:T(4,128)S(1)}, f32[4,128]{1,0:T(4,128)S(1)}, u32[]{:S(2)}, u32[]{:S(2)}) collective-permute-start(f32[4,128]{1,0:T(4,128)S(1)} %pad_maximum_fusion.4.meta_ref), channel_id=1, source_target_pairs={{0,24},{4,28},{8,16},{12,20},{24,0},{28,4},{16,8},{20,12},{1,25},{... | collective-permute-start | bytes 6152 | tf_op jit(solution)/shard_map/ppermute | solution.py:354
  7.0 25.8 %collective-permute-start.2 = (bf16[128,2048]{1,0:T(8,128)(2,1)}, bf16[128,2048]{1,0:T(8,128)(2,1)S(1)}, u32[]{:S(2)}, u32[]{:S(2)}) collective-permute-start(bf16[128,2048]{1,0:T(8,128)(2,1)} %x_ref.1), channel_id=1, source_target_pairs={{0,8},{4,12},{8,24},{12,28},{24,16},{28,20},{16,0},{20,4},{1,9},{5... | collective-permute-start | bytes 1572872 | tf_op jit(solution)/shard_map/ppermute | solution.py:354
  7.1 25.8 %collective-permute-start.3 = (bf16[128,2048]{1,0:T(8,128)(2,1)}, bf16[128,2048]{1,0:T(8,128)(2,1)S(1)}, u32[]{:S(2)}, u32[]{:S(2)}) collective-permute-start(bf16[128,2048]{1,0:T(8,128)(2,1)} %d_ref.1), channel_id=1, source_target_pairs={{0,8},{4,12},{8,24},{12,28},{24,16},{28,20},{16,0},{20,4},{1,9},{5... | collective-permute-start | bytes 1572872 | tf_op jit(solution)/shard_map/ppermute | solution.py:354
  8.3 24.6 %collective-permute-start.1 = (f32[4,128]{1,0:T(4,128)S(1)}, f32[4,128]{1,0:T(4,128)S(1)}, u32[]{:S(2)}, u32[]{:S(2)}) collective-permute-start(f32[4,128]{1,0:T(4,128)S(1)} %pad_maximum_fusion.4.meta_ref), channel_id=1, source_target_pairs={{0,8},{4,12},{8,24},{12,28},{24,16},{28,20},{16,0},{20,4},{1,9},{5... | collective-permute-start | bytes 6152 | tf_op jit(solution)/shard_map/ppermute | solution.py:354
  13.2 29.9 %collective-permute-start = (bf16[2,64,2048]{2,1,0:T(8,128)(2,1)}, bf16[2,64,2048]{2,1,0:T(8,128)(2,1)S(1)}, u32[]{:S(2)}, u32[]{:S(2)}) collective-permute-start(bf16[2,64,2048]{2,1,0:T(8,128)(2,1)} %get-tuple-element.36), channel_id=1, source_target_pairs={{0,4},{4,0},{8,12},{12,8},{16,20},{20,16},{24,28},{28,24},{1,5},{5... | collective-permute-start | bytes 1572872 | tf_op jit(solution)/shard_map/ppermute | solution.py:362
  32.8 61.9 %collective-permute-start.6 = (f32[4,128]{1,0:T(4,128)}, f32[4,128]{1,0:T(4,128)S(1)}, u32[]{:S(2)}, u32[]{:S(2)}) collective-permute-start(f32[4,128]{1,0:T(4,128)} %copy-done.29), channel_id=1, source_target_pairs={{0,16},{4,20},{8,0},{12,4},{24,8},{28,12},{16,24},{20,28},{1,17},{... | collective-permute-start | bytes 6152 | tf_op jit(solution)/shard_map/ppermute | solution.py:354
  38.7 33.4 %collective-permute-start.4 = (bf16[2,64,2048]{2,1,0:T(8,128)(2,1)}, bf16[2,64,2048]{2,1,0:T(8,128)(2,1)S(1)}, u32[]{:S(2)}, u32[]{:S(2)}) collective-permute-start(bf16[2,64,2048]{2,1,0:T(8,128)(2,1)} %get-tuple-element.38), channel_id=1, source_target_pairs={{0,4},{4,0},{8,12},{12,8},{16,20},{20,16},{24,28},{28,24},{1,5},{5... | collective-permute-start | bytes 1572872 | tf_op jit(solution)/shard_map/ppermute | solution.py:362
  40.2 16.0 %collective-permute-start.7 = (bf16[128,2048]{1,0:T(8,128)(2,1)}, bf16[128,2048]{1,0:T(8,128)(2,1)S(1)}, u32[]{:S(2)}, u32[]{:S(2)}) collective-permute-start(bf16[128,2048]{1,0:T(8,128)(2,1)} %copy-done.19), channel_id=1, source_target_pairs={{0,8},{4,12},{8,24},{12,28},{24,16},{28,20},{16,0},{20,4},{1,9},{5... | collective-permute-start | bytes 1572872 | tf_op jit(solution)/shard_map/ppermute | solution.py:354
  43.2 21.5 %collective-permute-start.9 = (bf16[128,2048]{1,0:T(8,128)(2,1)}, bf16[128,2048]{1,0:T(8,128)(2,1)S(1)}, u32[]{:S(2)}, u32[]{:S(2)}) collective-permute-start(bf16[128,2048]{1,0:T(8,128)(2,1)} %copy-done.20), channel_id=1, source_target_pairs={{0,8},{4,12},{8,24},{12,28},{24,16},{28,20},{16,0},{20,4},{1,9},{5... | collective-permute-start | bytes 1572872 | tf_op jit(solution)/shard_map/ppermute | solution.py:354
  43.6 97.6 %collective-permute-start.25 = (bf16[128,2048]{1,0:T(8,128)(2,1)S(1)}, bf16[128,2048]{1,0:T(8,128)(2,1)S(1)}, u32[]{:S(2)}, u32[]{:S(2)}) collective-permute-start(bf16[128,2048]{1,0:T(8,128)(2,1)S(1)} %pad_maximum_fusion), channel_id=1, source_target_pairs={{0,2},{1,3},{2,0},{3,1},{4,6},{5,7},{6,4},{7,5},{8,10},{9,11},{10,... | collective-permute-start | bytes 1572872 | tf_op jit(solution)/shard_map/ppermute | solution.py:365
  69.7 34.1 %collective-permute-start.12 = (bf16[2,64,2048]{2,1,0:T(8,128)(2,1)}, bf16[2,64,2048]{2,1,0:T(8,128)(2,1)S(1)}, u32[]{:S(2)}, u32[]{:S(2)}) collective-permute-start(bf16[2,64,2048]{2,1,0:T(8,128)(2,1)} %get-tuple-element.43), channel_id=1, source_target_pairs={{0,4},{4,0},{8,12},{12,8},{16,20},{20,16},{24,28},{28,24},{1,5},{5... | collective-permute-start | bytes 1572872 | tf_op jit(solution)/shard_map/ppermute | solution.py:362
  70.2 26.1 %collective-permute-start.8 = (bf16[128,2048]{1,0:T(8,128)(2,1)}, bf16[128,2048]{1,0:T(8,128)(2,1)S(1)}, u32[]{:S(2)}, u32[]{:S(2)}) collective-permute-start(bf16[128,2048]{1,0:T(8,128)(2,1)} %copy-done.21), channel_id=1, source_target_pairs={{0,8},{4,12},{8,24},{12,28},{24,16},{28,20},{16,0},{20,4},{1,9},{5... | collective-permute-start | bytes 1572872 | tf_op jit(solution)/shard_map/ppermute | solution.py:354
  72.1 24.8 %collective-permute-start.10 = (bf16[128,2048]{1,0:T(8,128)(2,1)}, bf16[128,2048]{1,0:T(8,128)(2,1)S(1)}, u32[]{:S(2)}, u32[]{:S(2)}) collective-permute-start(bf16[128,2048]{1,0:T(8,128)(2,1)} %copy-done.22), channel_id=1, source_target_pairs={{0,8},{4,12},{8,24},{12,28},{24,16},{28,20},{16,0},{20,4},{1,9},{5... | collective-permute-start | bytes 1572872 | tf_op jit(solution)/shard_map/ppermute | solution.py:354
  94.8 47.7 %collective-permute-start.26 = (bf16[128,2048]{1,0:T(8,128)(2,1)S(1)}, bf16[128,2048]{1,0:T(8,128)(2,1)S(1)}, u32[]{:S(2)}, u32[]{:S(2)}) collective-permute-start(bf16[128,2048]{1,0:T(8,128)(2,1)S(1)} %pad_maximum_fusion.1), channel_id=1, source_target_pairs={{0,2},{1,3},{2,0},{3,1},{4,6},{5,7},{6,4},{7,5},{8,10},{9,11},{10,... | collective-permute-start | bytes 1572872 | tf_op jit(solution)/shard_map/ppermute | solution.py:365
  96.3 47.0 %collective-permute-start.23 = (bf16[1408,256]{1,0:T(8,128)(2,1)}, bf16[1408,256]{1,0:T(8,128)(2,1)S(1)}, u32[]{:S(2)}, u32[]{:S(2)}) collective-permute-start(bf16[1408,256]{1,0:T(8,128)(2,1)} %get-tuple-element.62), channel_id=1, source_target_pairs={{0,2},{1,3},{2,0},{3,1},{4,6},{5,7},{6,4},{7,5},{8,10},{9,11},{10,... | collective-permute-start | bytes 2162696 | tf_op jit(solution)/shard_map/ppermute | solution.py:365
  134.6 36.3 %collective-permute-start.24 = (bf16[1408,256]{1,0:T(8,128)(2,1)}, bf16[1408,256]{1,0:T(8,128)(2,1)S(1)}, u32[]{:S(2)}, u32[]{:S(2)}) collective-permute-start(bf16[1408,256]{1,0:T(8,128)(2,1)} %get-tuple-element.63), channel_id=1, source_target_pairs={{0,2},{1,3},{2,0},{3,1},{4,6},{5,7},{6,4},{7,5},{8,10},{9,11},{10,... | collective-permute-start | bytes 2162696 | tf_op jit(solution)/shard_map/ppermute | solution.py:365
  141.0 61.2 %collective-permute-start.21 = (bf16[352,2048]{1,0:T(8,128)(2,1)}, bf16[352,2048]{1,0:T(8,128)(2,1)S(1)}, u32[]{:S(2)}, u32[]{:S(2)}) collective-permute-start(bf16[352,2048]{1,0:T(8,128)(2,1)} %get-tuple-element.59), channel_id=1, source_target_pairs={{0,1},{1,0},{2,3},{3,2},{4,5},{5,4},{6,7},{7,6},{8,9},{9,8},{10,11... | collective-permute-start | bytes 4325384 | tf_op jit(solution)/shard_map/ppermute | solution.py:365
  141.2 22.2 %collective-permute-start.27 = (bf16[128,2048]{1,0:T(8,128)(2,1)S(1)}, bf16[128,2048]{1,0:T(8,128)(2,1)S(1)}, u32[]{:S(2)}, u32[]{:S(2)}) collective-permute-start(bf16[128,2048]{1,0:T(8,128)(2,1)S(1)} %pad_maximum_fusion.2), channel_id=1, source_target_pairs={{0,2},{1,3},{2,0},{3,1},{4,6},{5,7},{6,4},{7,5},{8,10},{9,11},{10,... | collective-permute-start | bytes 1572872 | tf_op jit(solution)/shard_map/ppermute | solution.py:365
  142.4 28.4 %collective-permute-start.28 = (bf16[128,2048]{1,0:T(8,128)(2,1)S(1)}, bf16[128,2048]{1,0:T(8,128)(2,1)S(1)}, u32[]{:S(2)}, u32[]{:S(2)}) collective-permute-start(bf16[128,2048]{1,0:T(8,128)(2,1)S(1)} %pad_maximum_fusion.3), channel_id=1, source_target_pairs={{0,2},{1,3},{2,0},{3,1},{4,6},{5,7},{6,4},{7,5},{8,10},{9,11},{10,... | collective-permute-start | bytes 1572872 | tf_op jit(solution)/shard_map/ppermute | solution.py:365
  182.1 72.1 %collective-permute-start.29 = (bf16[2,352,2048]{2,1,0:T(8,128)(2,1)}, bf16[2,352,2048]{2,1,0:T(8,128)(2,1)S(1)}, u32[]{:S(2)}, u32[]{:S(2)}) collective-permute-start(bf16[2,352,2048]{2,1,0:T(8,128)(2,1)} %get-tuple-element.65), channel_id=1, source_target_pairs={{0,1},{1,0},{2,3},{3,2},{4,5},{5,4},{6,7},{7,6},{8,9},{9,8},{10,11... | collective-permute-start | bytes 8650760 | tf_op jit(solution)/shard_map/ppermute | solution.py:365
  195.2 14.6 %collective-permute-start.17 = (bf16[128,2048]{1,0:T(8,128)(2,1)}, bf16[128,2048]{1,0:T(8,128)(2,1)S(1)}, u32[]{:S(2)}, u32[]{:S(2)}) collective-permute-start(bf16[128,2048]{1,0:T(8,128)(2,1)} %merge.4), channel_id=1, source_target_pairs={{0,8},{4,12},{8,24},{12,28},{24,16},{28,20},{16,0},{20,4},{1,9},{5... | collective-permute-start | bytes 1572872 | tf_op jit(solution)/shard_map/ppermute | solution.py:354
  202.1 58.6 %collective-permute-start.20 = (bf16[352,2048]{1,0:T(8,128)(2,1)}, bf16[352,2048]{1,0:T(8,128)(2,1)S(1)}, u32[]{:S(2)}, u32[]{:S(2)}) collective-permute-start(bf16[352,2048]{1,0:T(8,128)(2,1)} %get-tuple-element.57), channel_id=1, source_target_pairs={{0,1},{1,0},{2,3},{3,2},{4,5},{5,4},{6,7},{7,6},{8,9},{9,8},{10,11... | collective-permute-start | bytes 4325384 | tf_op jit(solution)/shard_map/ppermute | solution.py:365
  203.9 56.8 %collective-permute-start.22 = (bf16[352,2048]{1,0:T(8,128)(2,1)}, bf16[352,2048]{1,0:T(8,128)(2,1)S(1)}, u32[]{:S(2)}, u32[]{:S(2)}) collective-permute-start(bf16[352,2048]{1,0:T(8,128)(2,1)} %add_convert_fusion), channel_id=1, source_target_pairs={{0,2},{1,3},{2,0},{3,1},{4,6},{5,7},{6,4},{7,5},{8,10},{9,11},{10,... | collective-permute-start | bytes 4325384 | tf_op jit(solution)/shard_map/ppermute | solution.py:365
  217.5 14.3 %collective-permute-start.18 = (bf16[128,2048]{1,0:T(8,128)(2,1)}, bf16[128,2048]{1,0:T(8,128)(2,1)S(1)}, u32[]{:S(2)}, u32[]{:S(2)}) collective-permute-start(bf16[128,2048]{1,0:T(8,128)(2,1)} %merge.5), channel_id=1, source_target_pairs={{0,8},{4,12},{8,24},{12,28},{24,16},{28,20},{16,0},{20,4},{1,9},{5... | collective-permute-start | bytes 1572872 | tf_op jit(solution)/shard_map/ppermute | solution.py:354
  (43 other events, 321.2 us)
